TPU v7x, 512 devices: a whole 4x8x8 slice. The times are simulated.
512 devices in a mesh: ctx: 128 (over z, y, core), tp: 4 (over x).
Axes of the slice: x: 4, y: 8, z: 8, core: 2. Of those that a mesh axis runs over, the one named last changes fastest.
Arguments:
- query_base: bfloat16 [16384, 3584], P('ctx', 'tp'), may hold values from -6 to 6
- key_base: bfloat16 [16384, 3584], P('ctx', 'tp'), may hold values from -6 to 6
- value_base: bfloat16 [16384, 3584], P('ctx', 'tp'), may hold values from -6 to 6
- adapter_activation: bfloat16 [16384, 128], P('ctx'), may hold values from -6 to 6
- adapter_up_weight: bfloat16 [2, 128, 3584], P(None, None, 'tp'), may hold values from -0.5 to 0.5
- output_grad: bfloat16 [16384, 3584], P('ctx', 'tp'), may hold values from -6 to 6
- stretch_doc: int32 [256], replicated, may hold values from 3 to 255, as said below
- doc_first: int32 [256], replicated, may hold values from 0 to 255, as said below
- slot_stretch: int32 [256], replicated, may hold values from 0 to 255, as said below
Outputs:
- grad_query: bfloat16 [16384, 3584], P('ctx', 'tp')
- grad_key: bfloat16 [16384, 3584], P('ctx', 'tp')
- grad_value: bfloat16 [16384, 3584], P('ctx', 'tp')
- grad_input: bfloat16 [16384, 128], P('ctx')
- grad_adapter: float32 [2, 128, 3584], P(None, None, 'tp')
Inputs may be any that keep to these rules, and one draw needn't show every extreme that they name: stretch_doc never falls along the slab; a document covers 1 to 4 consecutive stretches, the first document exactly 4, the last stretch a document of its own; a document's id is the slab index of its last stretch. doc_first[c] is the smallest stretch index with the document id of stretch c. `slot_stretch`: each stretch is held in exactly one slot; slot s lies on ctx index s // 2; the ctx indices of each aligned group of 2 hold exactly that group's 4 consecutive stretches.
All inputs are finite; a program needn't handle non-finite values.
Results may differ from a plain program's by a relative error of at most 0.012.
The roundings to bfloat16 on the way count: a program that leaves them out, or rounds other values in their place, can miss the bound.
Values may be sent and summed in bfloat16 or wider, within the bound.
A program may use at most 64 MiB of HBM per device.

v0:
```python
import jax
import jax.numpy as jnp
from jax import lax
from jax.sharding import PartitionSpec as P

HEAD_WIDTH = 224
STRETCHES_DEV = 2
GROUP_SIZE = 2


masked_fill = -1e30


def passed_along(array, axis, by):
    count = lax.axis_size(axis)
    pairs = [(i, i + by) for i in range(count) if 0 <= i + by < count]
    return lax.ppermute(array, axis, pairs)


def lookup(table, wanted):
    places = jnp.arange(table.shape[0], dtype=jnp.int32)
    return jnp.sum(jnp.where(places[None, :] == wanted[:, None], table[None, :], 0), axis=1)


def adapted(base, adapter_activation, adapter_piece):
    update = jnp.dot(adapter_activation, adapter_piece, preferred_element_type=jnp.float32)
    return (base.astype(jnp.float32) + update).astype(jnp.bfloat16)


def visibility(own_stretches, other_stretches, source_ok, stretch_doc, doc_first, stretch_len):
    own_doc = lookup(stretch_doc, own_stretches)
    own_first = lookup(doc_first, own_stretches)
    other_doc = lookup(stretch_doc, other_stretches)
    earlier = (
        (other_stretches[None, :] < own_stretches[:, None])
        & (other_stretches[None, :] >= own_first[:, None])
        & (other_doc[None, :] == own_doc[:, None])
        & source_ok
    )
    same = (other_stretches[None, :] == own_stretches[:, None]) & source_ok
    inside = jnp.arange(stretch_len, dtype=jnp.int32)
    lower = inside[:, None] >= inside[None, :]
    full = earlier[:, None, :, None] | same[:, None, :, None] & lower[None, :, None, :]
    row_count = own_stretches.shape[0] * stretch_len
    return (
        full.reshape(row_count, other_stretches.shape[0] * stretch_len),
        jnp.any(earlier | same),
    )


def masked_scores(query_heads, key_heads, visible, score_scale):
    raw = (
        jnp.einsum("qhe,khe->hqk", query_heads, key_heads, preferred_element_type=jnp.float32)
        * score_scale
    )
    return jnp.where(visible[None], raw, masked_fill)


def body(
    query_base,
    key_base,
    value_base,
    adapter_activation,
    adapter_up_weight,
    output_grad,
    stretch_doc,
    doc_first,
    slot_stretch,
):
    row_count, columns = query_base.shape
    head_local = columns // HEAD_WIDTH
    stretch_len = row_count // STRETCHES_DEV
    score_scale = HEAD_WIDTH ** (-0.5)
    ctx_count = lax.axis_size("ctx")
    device_at = lax.axis_index("ctx")

    def split_heads(values):
        return values.reshape(values.shape[0], head_local, HEAD_WIDTH)

    query = adapted(query_base, adapter_activation, adapter_up_weight[0])
    value = adapted(value_base, adapter_activation, adapter_up_weight[1])
    own_stretches = lax.dynamic_slice_in_dim(slot_stretch, device_at * STRETCHES_DEV, STRETCHES_DEV)
    offsets = [shift_by for shift_by in range(1 - GROUP_SIZE, 2 * GROUP_SIZE) if shift_by != 0]
    local_pair = jnp.stack([key_base, value])
    sources = [device_at - shift_by for shift_by in [0] + offsets]

    def receive():
        return [local_pair] + [passed_along(local_pair, "ctx", shift_by) for shift_by in offsets]

    masks = []
    for source in sources:
        source_ok = (source >= 0) & (source < ctx_count)
        other = lax.dynamic_slice_in_dim(
            slot_stretch, jnp.clip(source, 0, ctx_count - 1) * STRETCHES_DEV, STRETCHES_DEV
        )
        masks.append(
            visibility(own_stretches, other, source_ok, stretch_doc, doc_first, stretch_len)
        )
    query_heads = split_heads(query)
    grad_heads = split_heads(output_grad)
    arrived = receive()
    piece_count = len(arrived)
    peak = jnp.full((head_local, row_count), masked_fill, jnp.float32)
    norm_sum = jnp.zeros((head_local, row_count), jnp.float32)
    for place in range(piece_count):
        visible, useful = masks[place]

        def gather_stats(running, pair=arrived[place], visible=visible):
            old_peak, old_sum = running
            logits = masked_scores(query_heads, split_heads(pair[0]), visible, score_scale)
            new_peak = jnp.maximum(old_peak, jnp.max(logits, axis=2))
            weights = jnp.where(visible[None], jnp.exp(logits - new_peak[..., None]), 0.0)
            return (new_peak, old_sum * jnp.exp(old_peak - new_peak) + jnp.sum(weights, axis=2))

        peak, norm_sum = lax.cond(useful, gather_stats, lambda running: running, (peak, norm_sum))

    def probabilities(key_heads, visible):
        logits = masked_scores(query_heads, key_heads, visible, score_scale)
        return (
            jnp.where(visible[None], jnp.exp(logits - peak[..., None]), 0.0) / norm_sum[..., None]
        )

    attended = jnp.zeros((row_count, head_local, HEAD_WIDTH), jnp.float32)
    for place in range(piece_count):
        visible, useful = masks[place]

        def add_values(summed, pair=arrived[place], visible=visible):
            probs_low = probabilities(split_heads(pair[0]), visible).astype(jnp.bfloat16)
            return summed + jnp.einsum(
                "hqk,khe->qhe", probs_low, split_heads(pair[1]), preferred_element_type=jnp.float32
            )

        attended = lax.cond(useful, add_values, lambda summed: summed, attended)
    row_dot = jnp.sum(grad_heads.astype(jnp.float32) * attended, axis=2).T
    query_gradient = jnp.zeros((row_count, head_local, HEAD_WIDTH), jnp.float32)
    returned = []
    for place in range(piece_count):
        visible, useful = masks[place]

        def piece_grads(summed, pair=arrived[place], visible=visible):
            key_heads = split_heads(pair[0])
            value_heads = split_heads(pair[1])
            probs = probabilities(key_heads, visible)
            probs_low = probs.astype(jnp.bfloat16)
            grad_probs = jnp.einsum(
                "qhe,khe->hqk", grad_heads, value_heads, preferred_element_type=jnp.float32
            )
            grad_scores = (probs * (grad_probs - row_dot[..., None])).astype(jnp.bfloat16)
            summed = summed + score_scale * jnp.einsum(
                "hqk,khe->qhe", grad_scores, key_heads, preferred_element_type=jnp.float32
            )
            key_terms = score_scale * jnp.einsum(
                "hqk,qhe->khe", grad_scores, query_heads, preferred_element_type=jnp.float32
            )
            value_terms = jnp.einsum(
                "hqk,qhe->khe", probs_low, grad_heads, preferred_element_type=jnp.float32
            )
            return (summed, jnp.stack([key_terms, value_terms]).reshape(2, row_count, columns))

        def skip_piece(summed):
            return (summed, jnp.zeros((2, row_count, columns), jnp.float32))

        query_gradient, terms = lax.cond(useful, piece_grads, skip_piece, query_gradient)
        returned.append(terms)
    pair_grad = returned[0]
    for place, shift_by in enumerate(offsets):
        sent_back = passed_along(returned[place + 1].astype(jnp.bfloat16), "ctx", -shift_by)
        pair_grad = pair_grad + sent_back.astype(jnp.float32)
    grad_query = query_gradient.reshape(row_count, columns).astype(jnp.bfloat16)
    grad_key = pair_grad[0].astype(jnp.bfloat16)
    grad_value = pair_grad[1].astype(jnp.bfloat16)
    input_part = jnp.einsum(
        "tc,rc->tr", grad_query, adapter_up_weight[0], preferred_element_type=jnp.float32
    ) + jnp.einsum(
        "tc,rc->tr", grad_value, adapter_up_weight[1], preferred_element_type=jnp.float32
    )
    grad_input = lax.psum(input_part, "tp").astype(jnp.bfloat16)
    adapter_part = jnp.stack(
        [
            jnp.einsum(
                "tr,tc->rc", adapter_activation, grad_query, preferred_element_type=jnp.float32
            ),
            jnp.einsum(
                "tr,tc->rc", adapter_activation, grad_value, preferred_element_type=jnp.float32
            ),
        ]
    )
    grad_adapter = lax.psum(adapter_part, "ctx")
    return (grad_query, grad_key, grad_value, grad_input, grad_adapter)


def solution(mesh):
    return jax.shard_map(
        body,
        mesh=mesh,
        in_specs=(
            P("ctx", "tp"),
            P("ctx", "tp"),
            P("ctx", "tp"),
            P("ctx", None),
            P(None, None, "tp"),
            P("ctx", "tp"),
            P(),
            P(),
            P(),
        ),
        out_specs=(
            P("ctx", "tp"),
            P("ctx", "tp"),
            P("ctx", "tp"),
            P("ctx", None),
            P(None, None, "tp"),
        ),
        check_vma=False,
    )
```

profile of v0, /device:TPU:1, one launch (start us, length us, event | category | flops | bytes accessed | tf_op | source)
XLA Modules:
  0.0 330.6 jit_solution(17091177899702221122)
XLA Ops:
  7.9 1.3 fusion.139
  10.0 5.6 %collective-permute-start.3 = (bf16[2,128,896]{2,1,0:T(8,128)(2,1)}, bf16[2,128,896]{2,1,0:T(8,128)(2,1)S(1)}, u32[]{:S(2)}, u32[]{:S(2)}) collective-permute-start(bf16[2,128,896]{2,1,0:T(8,128)(2,1)} %pad_maximum_fusion.6), channel_id=1, source_target_pairs={{0,12},{4,16},{8,20},{12,24},{16,28},{20,32},{24,36},{28,40},{32,4... | collective-permute-start | bytes 1376264 | tf_op jit(solution)/shard_map/ppermute | solution.py:17
  15.7 3.2 collective-permute-start.2
  18.9 2.2 collective-permute-start.1
  21.1 2.2 collective-permute-start
  31.0 2.1 conditional.15
  33.1 12.9 %collective-permute-done.1 = bf16[2,128,896]{2,1,0:T(8,128)(2,1)S(1)} collective-permute-done((bf16[2,128,896]{2,1,0:T(8,128)(2,1)}, bf16[2,128,896]{2,1,0:T(8,128)(2,1)S(1)}, u32[]{:S(2)}, u32[]{:S(2)}) %collective-permute-start.1) | collective-permute-done | bytes 458784 | tf_op jit(solution)/shard_map/ppermute | solution.py:17
  46.0 4.5 %conditional.17 = ((f32[4,128]{1,0:T(4,128)}, f32[4,128]{1,0:T(4,128)S(1)})) conditional(s32[]{:T(128)} %convert_element_type.132, (f32[4,128]{1,0:T(4,128)}, f32[4,128]{1,0:T(4,128)S(1)}) %get-tuple-element.771, (pred[2,64,2,64]{3,2,1,0:T(4,128)(4,1)S(1)}, bf16[2,128,896]{2,1,0:T(8,128)(2,1)S(1)}, bf16[128,4,224]{0,2,1:T(8,128)(2,1)S(1)}, ...), branch_computations={%region_20.21_spmd, %region_21.24_spmd} | conditional | flops 29754368 | bytes 2713648 | solution.py:115
  50.5 3.4 %conditional.20 = (f32[128,4,224]{0,2,1:T(8,128)}) conditional(s32[]{:T(128)} %convert_element_type.134, () %tuple.117, (pred[2,64,2,64]{3,2,1,0:T(4,128)(4,1)S(1)}, bf16[128,896]{1,0:T(8,128)(2,1)S(1)}, bf16[128,4,224]{0,2,1:T(8,128)(2,1)S(1)}, f32[4,128]{1,0:T(4,128)}, f32[4,128]{1,0:T(4,128)S(1)}, ...), branch_computations={%region_32.33_spmd, %region_33.34_spmd} | conditional | flops 59113472 | bytes 2117640 | solution.py:133
  51.7 2.2 convolution_bitcast_fusion
  53.9 3.7 %conditional.22 = (f32[128,4,224]{0,2,1:T(8,128)}) conditional(s32[]{:T(128)} %convert_element_type.132, f32[128,4,224]{0,2,1:T(8,128)} %get-tuple-element.776, (pred[2,64,2,64]{3,2,1,0:T(4,128)(4,1)S(1)}, bf16[2,128,896]{2,1,0:T(8,128)(2,1)S(1)}, bf16[128,4,224]{0,2,1:T(8,128)(2,1)S(1)}, f32[4,128]{1,0:T(4,128)}, f32[4,128]{1,0:T(4,128)S(1)}, ...), branch_computations={%region_36.37_spmd, %region_37.38_spmd} | conditional | flops 59228160 | bytes 3493896 | solution.py:133
  55.1 2.5 fusion.36
  58.7 4.7 %conditional.25 = (f32[128,4,224]{0,2,1:T(8,128)S(1)}, f32[2,128,896]{2,1,0:T(8,128)}) conditional(s32[]{:T(128)} %convert_element_type.134, () %tuple.110, (pred[2,64,2,64]{3,2,1,0:T(4,128)(4,1)S(1)}, bf16[128,896]{1,0:T(8,128)(2,1)S(1)}, bf16[128,4,224]{0,2,1:T(8,128)(2,1)S(1)}, f32[4,128]{1,0:T(4,128)}, f32[4,128]{1,0:T(4,128)S(1)}, ...), branch_computations={%region_43.44_spmd, %region_44.45_spmd} | conditional | flops 147849216 | bytes 9721900 | solution.py:163
  64.5 2.4 conditional.27
  70.1 1.3 collective-permute-start.7
  71.4 1.3 collective-permute-start.6
  72.7 1.9 collective-permute-start.5
  74.6 3.6 %collective-permute-start.4 = (bf16[2,128,896]{2,1,0:T(8,128)(2,1)}, bf16[2,128,896]{2,1,0:T(8,128)(2,1)S(1)}, u32[]{:S(2)}, u32[]{:S(2)}) collective-permute-start(bf16[2,128,896]{2,1,0:T(8,128)(2,1)} %copy.113), channel_id=1, source_target_pairs={{0,4},{4,8},{8,12},{12,16},{16,20},{20,24},{24,28},{28,32},{32,36}... | collective-permute-start | bytes 1376264 | tf_op jit(solution)/shard_map/ppermute | solution.py:17
  79.3 10.2 %collective-permute-done.7 = bf16[2,128,896]{2,1,0:T(8,128)(2,1)S(1)} collective-permute-done((bf16[2,128,896]{2,1,0:T(8,128)(2,1)}, bf16[2,128,896]{2,1,0:T(8,128)(2,1)S(1)}, u32[]{:S(2)}, u32[]{:S(2)}) %collective-permute-start.7) | collective-permute-done | bytes 458784 | tf_op jit(solution)/shard_map/ppermute | solution.py:17
  90.6 4.5 %collective-permute-done.5 = bf16[2,128,896]{2,1,0:T(8,128)(2,1)S(1)} collective-permute-done((bf16[2,128,896]{2,1,0:T(8,128)(2,1)}, bf16[2,128,896]{2,1,0:T(8,128)(2,1)S(1)}, u32[]{:S(2)}, u32[]{:S(2)}) %collective-permute-start.5) | collective-permute-done | bytes 458784 | tf_op jit(solution)/shard_map/ppermute | solution.py:17
  95.9 1.6 convert_add_fusion
  101.0 13.2 %psum.14 = bf16[128,128]{1,0:T(8,128)(2,1)} all-reduce(f32[128,128]{1,0:T(8,128)S(1)} %convolution_add_fusion.2), channel_id=1, replica_groups=mesh['ctx'=128,'tp'=4] {'tp'}, use_global_device_ids=true, to_apply=%region_53.54 | all-reduce | flops 16384 | bytes 98304 | tf_op jit(solution)/shard_map/psum | solution.py:177
  114.1 207.3 %all-reduce.2.cloned.1.call-done = f32[2,128,896]{1,2,0:T(8,128)} async-done(((f32[2,128,896]{1,2,0:T(8,128)}), f32[2,128,896]{1,2,0:T(8,128)}) %all-reduce.2.cloned.1.call-update) | async-done | bytes 917520 | tf_op jit(solution)/shard_map/psum | solution.py:188
  321.4 2.4 copy.119
  (121 shorter events, 33.6 us)
Async XLA Ops:
  7.2 2.0 copy-start.1
  7.2 314.2 %all-reduce.2.cloned.1.call-start = ((), (), s32[]{:S(2)}) async-start(), calls=%async_computation | async-start | bytes 1835008 | tf_op jit(solution)/shard_map/psum | solution.py:188
  9.2 14.1 %copy-start.3 = (bf16[2,128,896]{2,1,0:T(8,128)(2,1)S(1)}, bf16[2,128,896]{2,1,0:T(8,128)(2,1)}, u32[]{:S(2)}) copy-start(bf16[2,128,896]{2,1,0:T(8,128)(2,1)} %param.43) | copy-start | bytes 1376260
  9.2 14.1 %copy-start.15 = (bf16[128,896]{1,0:T(8,128)(2,1)S(1)}, bf16[128,896]{1,0:T(8,128)(2,1)}, u32[]{:S(2)}) copy-start(bf16[128,896]{1,0:T(8,128)(2,1)} %param.39) | copy-start | bytes 688132
  10.0 40.4 %collective-permute-start.3 = (bf16[2,128,896]{2,1,0:T(8,128)(2,1)}, bf16[2,128,896]{2,1,0:T(8,128)(2,1)S(1)}, u32[]{:S(2)}, u32[]{:S(2)}) collective-permute-start(bf16[2,128,896]{2,1,0:T(8,128)(2,1)} %pad_maximum_fusion.6), channel_id=1, source_target_pairs={{0,12},{4,16},{8,20},{12,24},{16,28},{20,32},{24,36},{28,40},{32,4... | collective-permute-start | bytes 1376264 | tf_op jit(solution)/shard_map/ppermute | solution.py:17
  15.7 34.8 %collective-permute-start.2 = (bf16[2,128,896]{2,1,0:T(8,128)(2,1)}, bf16[2,128,896]{2,1,0:T(8,128)(2,1)S(1)}, u32[]{:S(2)}, u32[]{:S(2)}) collective-permute-start(bf16[2,128,896]{2,1,0:T(8,128)(2,1)} %pad_maximum_fusion.6), channel_id=1, source_target_pairs={{0,8},{4,12},{8,16},{12,20},{16,24},{20,28},{24,32},{28,36},{32,40... | collective-permute-start | bytes 1376264 | tf_op jit(solution)/shard_map/ppermute | solution.py:17
  18.9 27.1 %collective-permute-start.1 = (bf16[2,128,896]{2,1,0:T(8,128)(2,1)}, bf16[2,128,896]{2,1,0:T(8,128)(2,1)S(1)}, u32[]{:S(2)}, u32[]{:S(2)}) collective-permute-start(bf16[2,128,896]{2,1,0:T(8,128)(2,1)} %pad_maximum_fusion.6), channel_id=1, source_target_pairs={{0,4},{4,8},{8,12},{12,16},{16,20},{20,24},{24,28},{28,32},{32,36}... | collective-permute-start | bytes 1376264 | tf_op jit(solution)/shard_map/ppermute | solution.py:17
  21.1 12.0 %collective-permute-start = (bf16[2,128,896]{2,1,0:T(8,128)(2,1)}, bf16[2,128,896]{2,1,0:T(8,128)(2,1)S(1)}, u32[]{:S(2)}, u32[]{:S(2)}) collective-permute-start(bf16[2,128,896]{2,1,0:T(8,128)(2,1)} %pad_maximum_fusion.6), channel_id=1, source_target_pairs={{4,0},{8,4},{12,8},{16,12},{20,16},{24,20},{28,24},{32,28},{36,32}... | collective-permute-start | bytes 1376264 | tf_op jit(solution)/shard_map/ppermute | solution.py:17
  29.3 0.9 copy-start.14
  30.9 19.6 %copy-start.10 = (pred[2,64,2,64]{3,2,1,0:T(4,128)(4,1)}, pred[2,64,2,64]{3,2,1,0:T(4,128)(4,1)S(1)}, u32[]{:S(2)}) copy-start(pred[2,64,2,64]{3,2,1,0:T(4,128)(4,1)S(1)} %get-tuple-element.712) | copy-start | bytes 49156
  31.0 22.9 %copy-start.9 = (pred[2,64,2,64]{3,2,1,0:T(4,128)(4,1)}, pred[2,64,2,64]{3,2,1,0:T(4,128)(4,1)S(1)}, u32[]{:S(2)}) copy-start(pred[2,64,2,64]{3,2,1,0:T(4,128)(4,1)S(1)} %get-tuple-element.709) | copy-start | bytes 49156
  31.0 22.9 %copy-start.7 = (pred[2,64,2,64]{3,2,1,0:T(4,128)(4,1)}, pred[2,64,2,64]{3,2,1,0:T(4,128)(4,1)S(1)}, u32[]{:S(2)}) copy-start(pred[2,64,2,64]{3,2,1,0:T(4,128)(4,1)S(1)} %get-tuple-element.710) | copy-start | bytes 49156
  31.0 26.6 %copy-start.5 = (pred[2,64,2,64]{3,2,1,0:T(4,128)(4,1)}, pred[2,64,2,64]{3,2,1,0:T(4,128)(4,1)S(1)}, u32[]{:S(2)}) copy-start(pred[2,64,2,64]{3,2,1,0:T(4,128)(4,1)S(1)} %get-tuple-element.711) | copy-start | bytes 49156
  47.2 0.9 slice-start.1
  57.6 1.1 copy-start.11
  59.2 1.0 copy-start.12
  63.5 1.0 copy-start.8
  66.9 1.0 copy-start.6
  70.1 19.4 %collective-permute-start.7 = (bf16[2,128,896]{2,1,0:T(8,128)(2,1)}, bf16[2,128,896]{2,1,0:T(8,128)(2,1)S(1)}, u32[]{:S(2)}, u32[]{:S(2)}) collective-permute-start(bf16[2,128,896]{2,1,0:T(8,128)(2,1)} %copy.117), channel_id=1, source_target_pairs={{12,0},{16,4},{20,8},{24,12},{28,16},{32,20},{36,24},{40,28},{44,3... | collective-permute-start | bytes 1376264 | tf_op jit(solution)/shard_map/ppermute | solution.py:17
  71.4 19.2 %collective-permute-start.6 = (bf16[2,128,896]{2,1,0:T(8,128)(2,1)}, bf16[2,128,896]{2,1,0:T(8,128)(2,1)S(1)}, u32[]{:S(2)}, u32[]{:S(2)}) collective-permute-start(bf16[2,128,896]{2,1,0:T(8,128)(2,1)} %copy.116), channel_id=1, source_target_pairs={{8,0},{12,4},{16,8},{20,12},{24,16},{28,20},{32,24},{36,28},{40,32... | collective-permute-start | bytes 1376264 | tf_op jit(solution)/shard_map/ppermute | solution.py:17
  72.7 22.4 %collective-permute-start.5 = (bf16[2,128,896]{2,1,0:T(8,128)(2,1)}, bf16[2,128,896]{2,1,0:T(8,128)(2,1)S(1)}, u32[]{:S(2)}, u32[]{:S(2)}) collective-permute-start(bf16[2,128,896]{2,1,0:T(8,128)(2,1)} %copy.115), channel_id=1, source_target_pairs={{4,0},{8,4},{12,8},{16,12},{20,16},{24,20},{28,24},{32,28},{36,32}... | collective-permute-start | bytes 1376264 | tf_op jit(solution)/shard_map/ppermute | solution.py:17
  74.6 20.5 %collective-permute-start.4 = (bf16[2,128,896]{2,1,0:T(8,128)(2,1)}, bf16[2,128,896]{2,1,0:T(8,128)(2,1)S(1)}, u32[]{:S(2)}, u32[]{:S(2)}) collective-permute-start(bf16[2,128,896]{2,1,0:T(8,128)(2,1)} %copy.113), channel_id=1, source_target_pairs={{0,4},{4,8},{8,12},{12,16},{16,20},{20,24},{24,28},{28,32},{32,36}... | collective-permute-start | bytes 1376264 | tf_op jit(solution)/shard_map/ppermute | solution.py:17
  98.2 2.5 copy-start.2
  99.4 1.0 copy-start.4
  (5 other events, 3.7 us)
Sparse Core Ops, SparseCore 0:
  99.6 221.7 all-reduce.1
where the time goes:
time: 332 us; the launch traced here: 331 us
  waiting for transfers between devices  236 us (71%)
  starting transfers between devices  21.3 us (6%)
  local copies, waits for them, and re-layouts  20.7 us (6%)
  between operations  17.7 us (5%)
  blocking collectives  13.2 us (4%)
  matrix products  12.5 us (4%)
  other arithmetic  8.96 us (3%)
    psum x1, waiting for transfers between devices, body(): grad_adapter = lax.psum(adapter_part, 'ctx')  207 us
    ppermute x8, waiting for transfers between devices, passed_along(): return lax.ppermute(array, axis, pairs)  28.7 us
    ppermute x8, starting transfers between devices, passed_along(): return lax.ppermute(array, axis, pairs)  21.3 us
    psum x1, blocking collectives, body(): grad_input = lax.psum(input_part, 'tp').astype(jnp.bfloat16)  13.2 us
    unnamed x39, local copies, waits for them, and re-layouts  8.06 us
  transfers between devices with their start and end apart: 9, of which 5 were waited for; matrix products, arithmetic and copies ran while one was open for 3% of the time, Pallas kernels for 0%

commit v1 on v0

v1 whole, which is shorter than its diff:
```python
import functools
import math

import jax
import jax.numpy as jnp
from jax import lax
from jax.experimental import pallas as pl
from jax.experimental.pallas import tpu as pltpu
from jax.sharding import PartitionSpec as P

HEAD = 224
PAD = 256
HEADS = 4
PAIR = 2 * PAD
ROWS = 128
STRETCH = 64
GROUP_ROWS = 2 * ROWS
WINDOW = 2 * GROUP_ROWS
SENT = 3 * STRETCH
RANK = 128
COLUMNS = HEADS * HEAD
SCALE = HEAD ** -0.5
FILL = -1e30

KEY, VALUE, QUERY, GRAD = range(4)
S_KEY, S_VALUE, S_QUERY, S_GRAD, S_ACT = range(5)
S_OUT = 5
S_INPUT = 8
S_ADAPTER = 9
S_NEXT = 11
S_BACK = 13
S_ALONG = 15
MESH = pl.DeviceIdType.MESH
F32 = jnp.float32
BF16 = jnp.bfloat16


def dot(a, b, contract):
    return lax.dot_general(a, b, ((contract[:1], contract[1:]), ((), ())), preferred_element_type=F32)


def padded(values):
    rows = values.shape[0]
    blank = jnp.zeros((rows, PAD - HEAD), values.dtype)
    parts = []
    for head in range(HEADS):
        parts += [values[:, head * HEAD:(head + 1) * HEAD], blank]
    return jnp.concatenate(parts, axis=1)


def unpadded(pairs):
    return jnp.concatenate(
        [pair[:, head * PAD:head * PAD + HEAD] for pair in pairs for head in range(2)], axis=1
    )


def kernel(
    side, n_tp,
    slot_ref, first_ref, q_hbm, k_hbm, v_hbm, a_hbm, w_hbm, g_hbm,
    out_ref, gi_ref, ga_ref,
    raw, act, weight, weight_pad, packed, sibling, act_sib, act_sorted,
    window_kv, sorted_qg, probs, probs_low, back_send, back_recv, own_kv,
    grads, sib_send, outs, gi_send, gi_sib, gi_along,
    part, scattered, crossed, gathered,
    load_sem, send_sem, recv_sem,
):
    me = lax.axis_index("ctx")
    tp = lax.axis_index("tp")
    core = lax.rem(me, 2)
    chip = lax.div(me, 2)
    y, z = lax.rem(chip, side), lax.div(chip, side)
    chips = side * side
    other = me + 1 - 2 * core
    after = lax.rem(chip + 1, chips) * 2 + core
    before = lax.rem(chip + chips - 1, chips) * 2 + core
    rows = RANK // side

    def along(axis, step):
        if axis == 0:
            return (z * side + lax.rem(y + step, side)) * 2 + core
        return (lax.rem(z + step, side) * side + y) * 2 + core

    def remote(src, dst, sem, ctx, x=None):
        return pltpu.make_async_remote_copy(
            src_ref=src, dst_ref=dst, send_sem=send_sem.at[sem], recv_sem=recv_sem.at[sem],
            device_id=(ctx, tp if x is None else x), device_id_type=MESH,
        )

    loads = [
        pltpu.make_async_copy(src, dst, load_sem.at[i])
        for i, (src, dst) in enumerate([
            (k_hbm, raw.at[KEY]), (a_hbm, act), (w_hbm, weight), (v_hbm, raw.at[VALUE]),
            (q_hbm, raw.at[QUERY]), (g_hbm, raw.at[GRAD]),
        ])
    ]
    for load in loads:
        load.start()

    barrier = pltpu.get_barrier_semaphore()

    def greet(ctx, x):
        pl.semaphore_signal(barrier, inc=1, device_id=(ctx, x), device_id_type=MESH)

    for device in (other, after, before):
        greet(device, tp)

    def greet_side(step, carry):
        greet(along(0, step), tp)
        greet(along(1, step), tp)
        return carry

    lax.fori_loop(1, side, greet_side, 0)

    def greet_tp(step, carry):
        greet(me, lax.rem(tp + step, n_tp))
        return carry

    lax.fori_loop(1, n_tp, greet_tp, 0)

    places = [
        slot_ref[2 * me] - 4 * chip, slot_ref[2 * me + 1] - 4 * chip,
        slot_ref[2 * other] - 4 * chip, slot_ref[2 * other + 1] - 4 * chip,
    ]

    def in_order(own, sib):
        slots = [own[:STRETCH], own[STRETCH:], sib[:STRETCH], sib[STRETCH:]]
        result = []
        for i in range(4):
            picked = slots[3]
            for j in (2, 1, 0):
                picked = jnp.where(places[j] == i, slots[j], picked)
            result.append(picked)
        return result

    def to_slots(values):
        result = []
        for j in range(4):
            picked = values[3 * STRETCH:]
            for i in (2, 1, 0):
                picked = jnp.where(places[j] == i, values[i * STRETCH:(i + 1) * STRETCH], picked)
            result.append(picked)
        return result

    def pack(kind, values):
        packed[kind, 0] = values[:, :PAIR]
        packed[kind, 1] = values[:, PAIR:]

    def to_sibling(kind, sem):
        return remote(packed.at[kind, 1 - core], sibling.at[kind], sem, other)

    loads[0].wait()
    pack(KEY, padded(raw[KEY]))
    pl.semaphore_wait(barrier, 3 + 2 * (side - 1) + n_tp - 1)
    sib_key = to_sibling(KEY, S_KEY)
    sib_key.start()
    loads[1].wait()
    sib_act = remote(act, act_sib, S_ACT, other)
    sib_act.start()
    loads[2].wait()
    for i in range(2):
        wide = padded(weight[i])
        weight_pad[i, 0] = wide[:, :PAIR]
        weight_pad[i, 1] = wide[:, PAIR:]

    def adapt(kind, i):
        wide = padded(raw[kind])
        for pair in range(2):
            update = dot(act[...], weight_pad[i, pair], (1, 0))
            base = wide[:, pair * PAIR:(pair + 1) * PAIR].astype(F32)
            packed[kind, pair] = (base + update).astype(BF16)

    loads[3].wait()
    adapt(VALUE, 1)
    sib_value = to_sibling(VALUE, S_VALUE)
    sib_value.start()

    def spread(kind):
        window_kv[kind, :STRETCH] = jnp.zeros((STRETCH, PAIR), BF16)
        for i, values in enumerate(in_order(packed[kind, core], sibling[kind])):
            window_kv[kind, GROUP_ROWS + i * STRETCH:GROUP_ROWS + (i + 1) * STRETCH] = values

    def to_next(kind):
        return remote(
            window_kv.at[kind, pl.ds(GROUP_ROWS + STRETCH, SENT)],
            window_kv.at[kind, pl.ds(STRETCH, SENT)], S_NEXT + kind, after,
        )

    sib_key.wait_recv()
    spread(KEY)
    next_key = to_next(KEY)
    next_key.start()
    sib_value.wait_recv()
    spread(VALUE)
    next_value = to_next(VALUE)
    next_value.start()

    loads[4].wait()
    adapt(QUERY, 0)
    sib_query = to_sibling(QUERY, S_QUERY)
    sib_query.start()
    loads[5].wait()
    pack(GRAD, padded(raw[GRAD]))
    sib_grad = to_sibling(GRAD, S_GRAD)
    sib_grad.start()

    sib_act.wait_recv()
    for i, values in enumerate(in_order(act[...], act_sib[...])):
        act_sorted[i * STRETCH:(i + 1) * STRETCH] = values
    for kind, copy in ((QUERY, sib_query), (GRAD, sib_grad)):
        copy.wait_recv()
        for i, values in enumerate(in_order(packed[kind, core], sibling[kind])):
            sorted_qg[kind - QUERY, i * STRETCH:(i + 1) * STRETCH] = values

    key_place = lax.broadcasted_iota(jnp.int32, (WINDOW, GROUP_ROWS), 0)
    query_place = lax.broadcasted_iota(jnp.int32, (1, GROUP_ROWS), 1)
    lowest = jnp.zeros((1, GROUP_ROWS), jnp.int32)
    for i in range(4):
        start = STRETCH * (first_ref[4 * chip + i] - 4 * chip + 4)
        lowest = jnp.where(query_place >= i * STRETCH, start, lowest)
    visible = (key_place >= lowest) & (key_place <= query_place + GROUP_ROWS)

    next_key.wait_recv()
    for head in range(2):
        lanes = slice(head * PAD, (head + 1) * PAD)
        scores = dot(window_kv[KEY, :, lanes], sorted_qg[0, :, lanes], (1, 1)) * SCALE
        scores = jnp.where(visible, scores, FILL)
        peak = jnp.max(scores, axis=0, keepdims=True)
        weights = jnp.exp(scores - peak)
        share = weights / jnp.sum(weights, axis=0, keepdims=True)
        probs[head] = share
        low = share.astype(BF16)
        probs_low[head] = low
        terms = dot(low, sorted_qg[1, :, lanes], (1, 0))
        back_send[VALUE, :, lanes] = terms[STRETCH:GROUP_ROWS].astype(BF16)
        own_kv[VALUE, :, lanes] = terms[GROUP_ROWS:]
    back_value = remote(back_send.at[VALUE], back_recv.at[VALUE], S_BACK + VALUE, before)
    back_value.start()

    next_value.wait_recv()
    for head in range(2):
        lanes = slice(head * PAD, (head + 1) * PAD)
        grad_probs = dot(window_kv[VALUE, :, lanes], sorted_qg[1, :, lanes], (1, 1))
        row_dot = jnp.sum(probs_low[head].astype(F32) * grad_probs, axis=0, keepdims=True)
        grad_scores = (probs[head] * (grad_probs - row_dot)).astype(BF16)
        terms = dot(grad_scores, sorted_qg[0, :, lanes], (1, 0)) * SCALE
        back_send[KEY, :, lanes] = terms[STRETCH:GROUP_ROWS].astype(BF16)
        own_kv[KEY, :, lanes] = terms[GROUP_ROWS:]
        summed = dot(grad_scores, window_kv[KEY, :, lanes], (0, 0)) * SCALE
        grads[0, :, lanes] = summed.astype(BF16)
    back_key = remote(back_send.at[KEY], back_recv.at[KEY], S_BACK + KEY, before)
    back_key.start()

    def along_sem(t, stage, step):
        return S_ALONG + (t * 3 + stage) * side + step

    position = [(y, z), (z, y)]

    def scatter(t, step):
        target = lax.rem(position[t][0] + step, side)
        return remote(part.at[t, target], scattered.at[t, step], along_sem(t, 0, step), along(t, step))

    def cross(t, step):
        mine = position[t][1]
        return remote(crossed.at[t, mine], crossed.at[t, mine], along_sem(t, 1, step), along(1 - t, step))

    def gather(t, step):
        mine = position[t][0]
        return remote(
            gathered.at[t, core, mine], gathered.at[t, core, mine], along_sem(t, 2, step), along(t, step)
        )

    def each(make, t, method):
        def run(step, carry):
            getattr(make(t, step), method)()
            return carry

        lax.fori_loop(1, side, run, 0)

    def adapter_terms(t, values):
        terms = dot(act_sorted[...], values, (0, 0)).astype(BF16)
        for j in range(side):
            part[t, j] = terms[j * rows:(j + 1) * rows]
        each(scatter, t, "start")

    def input_terms(t, values):
        return dot(values, weight_pad[t, core], (1, 1))

    def hand_out(t, slots):
        outs[t, core, :STRETCH] = slots[0]
        outs[t, core, STRETCH:] = slots[1]
        sib_send[t, :STRETCH] = slots[2]
        sib_send[t, STRETCH:] = slots[3]
        copy = remote(sib_send.at[t], outs.at[t, core], S_OUT + t, other)
        copy.start()
        return copy

    adapter_terms(0, grads[0])
    input_part = input_terms(0, grads[0])
    out_query = hand_out(0, to_slots(grads[0]))

    def add_back(kind):
        mine = own_kv[kind]
        return jnp.concatenate(
            [mine[:STRETCH], mine[STRETCH:] + back_recv[kind].astype(F32)], axis=0
        ).astype(BF16)

    back_value.wait_recv()
    grads[1] = add_back(VALUE)
    adapter_terms(1, grads[1])
    input_slots = to_slots(input_part + input_terms(1, grads[1]))
    gi_send[:STRETCH] = input_slots[2]
    gi_send[STRETCH:] = input_slots[3]
    sib_input = remote(gi_send, gi_sib, S_INPUT, other)
    sib_input.start()
    out_value = hand_out(2, to_slots(grads[1]))

    for t in range(2):
        each(scatter, t, "wait_recv")
        total = part[t, position[t][0]].astype(F32)
        for step in range(1, side):
            total = total + scattered[t, step].astype(F32)
        crossed[t, position[t][1]] = total.astype(BF16)
        each(cross, t, "start")

    sib_input.wait_recv()
    gi_along[tp, :STRETCH] = input_slots[0] + gi_sib[:STRETCH]
    gi_along[tp, STRETCH:] = input_slots[1] + gi_sib[STRETCH:]

    def tp_copy(step):
        return remote(
            gi_along.at[tp], gi_along.at[tp], S_ALONG + 6 * side + step, me, lax.rem(tp + step, n_tp)
        )

    def each_tp(method):
        def run(step, carry):
            getattr(tp_copy(step), method)()
            return carry

        lax.fori_loop(1, n_tp, run, 0)

    each_tp("start")

    for t in range(2):
        each(cross, t, "wait_recv")
        total = crossed[t, 0].astype(F32)
        for step in range(1, side):
            total = total + crossed[t, step].astype(F32)
        gathered[t, core, position[t][0]] = total.astype(BF16)
        each(gather, t, "start")

    back_key.wait_recv()
    out_key = hand_out(1, to_slots(add_back(KEY)))

    each_tp("wait_recv")
    total = gi_along[0]
    for x in range(1, n_tp):
        total = total + gi_along[x]
    gi_ref[...] = total.astype(BF16)

    sib_adapter = []
    for t in range(2):
        each(gather, t, "wait_recv")
        copy = remote(gathered.at[t, core], gathered.at[t, core], S_ADAPTER + t, other)
        copy.start()
        sib_adapter.append(copy)

    for copy in (out_query, out_value, out_key):
        copy.wait_recv()
    out_ref[...] = outs[...]
    for copy in sib_adapter:
        copy.wait_recv()
    ga_ref[...] = gathered[...]

    for copy in (
        sib_key, sib_act, sib_value, next_key, next_value, sib_query, sib_grad, back_value, back_key,
        out_query, out_value, out_key, sib_input, *sib_adapter,
    ):
        copy.wait_send()
    for t in range(2):
        each(scatter, t, "wait_send")
        each(cross, t, "wait_send")
        each(gather, t, "wait_send")
    each_tp("wait_send")


def finish(out_ref, ga_ref, q_ref, k_ref, v_ref, adapter_ref):
    for i, ref in enumerate((q_ref, k_ref, v_ref)):
        ref[...] = unpadded([out_ref[i, 0], out_ref[i, 1]])
    for i in range(2):
        adapter_ref[i] = unpadded([ga_ref[i, 0].astype(F32), ga_ref[i, 1].astype(F32)])


def body(
    query_base, key_base, value_base, adapter_activation, adapter_up_weight, output_grad,
    stretch_doc, doc_first, slot_stretch,
):
    n_tp = lax.axis_size("tp")
    side = math.isqrt(lax.axis_size("ctx") // 2)
    rows = RANK // side
    copies = S_ALONG + 6 * side + n_tp
    anywhere = pl.BlockSpec(memory_space=pl.ANY)
    vmem = pl.BlockSpec(memory_space=pltpu.VMEM)
    smem = pl.BlockSpec(memory_space=pltpu.SMEM)

    def block(*shape, dtype=BF16):
        return pltpu.VMEM(shape, dtype)

    outs, grad_input, adapter = pl.pallas_call(
        functools.partial(kernel, side, n_tp),
        out_shape=(
            jax.ShapeDtypeStruct((3, 2, ROWS, PAIR), BF16),
            jax.ShapeDtypeStruct((ROWS, RANK), BF16),
            jax.ShapeDtypeStruct((2, 2, side, rows, PAIR), BF16),
        ),
        in_specs=[smem, smem] + [anywhere] * 6,
        out_specs=(vmem, vmem, vmem),
        scratch_shapes=[
            block(4, ROWS, COLUMNS),
            block(ROWS, RANK),
            block(2, RANK, COLUMNS),
            block(2, 2, RANK, PAIR),
            block(4, 2, ROWS, PAIR),
            block(4, ROWS, PAIR),
            block(ROWS, RANK),
            block(GROUP_ROWS, RANK),
            block(2, WINDOW, PAIR),
            block(2, GROUP_ROWS, PAIR),
            block(2, WINDOW, GROUP_ROWS, dtype=F32),
            block(2, WINDOW, GROUP_ROWS),
            block(2, SENT, PAIR),
            block(2, SENT, PAIR),
            block(2, GROUP_ROWS, PAIR, dtype=F32),
            block(2, GROUP_ROWS, PAIR),
            block(3, ROWS, PAIR),
            block(3, 2, ROWS, PAIR),
            block(ROWS, RANK, dtype=F32),
            block(ROWS, RANK, dtype=F32),
            block(n_tp, ROWS, RANK, dtype=F32),
            block(2, side, rows, PAIR),
            block(2, side, rows, PAIR),
            block(2, side, rows, PAIR),
            block(2, 2, side, rows, PAIR),
            pltpu.SemaphoreType.DMA((6,)),
            pltpu.SemaphoreType.DMA((copies,)),
            pltpu.SemaphoreType.DMA((copies,)),
        ],
        compiler_params=pltpu.CompilerParams(
            collective_id=0, has_side_effects=True, vmem_limit_bytes=48 * 2**20
        ),
    )(
        slot_stretch, doc_first, query_base, key_base, value_base, adapter_activation,
        adapter_up_weight, output_grad,
    )
    grad_query, grad_key, grad_value, grad_adapter = pl.pallas_call(
        finish,
        out_shape=(
            jax.ShapeDtypeStruct((ROWS, COLUMNS), BF16),
            jax.ShapeDtypeStruct((ROWS, COLUMNS), BF16),
            jax.ShapeDtypeStruct((ROWS, COLUMNS), BF16),
            jax.ShapeDtypeStruct((2, RANK, COLUMNS), F32),
        ),
        in_specs=[vmem, vmem],
        out_specs=(vmem,) * 4,
        compiler_params=pltpu.CompilerParams(vmem_limit_bytes=48 * 2**20),
    )(outs, adapter.reshape(2, 2, RANK, PAIR))
    return grad_query, grad_key, grad_value, grad_input, grad_adapter


def solution(mesh):
    return jax.shard_map(
        body,
        mesh=mesh,
        in_specs=(
            P("ctx", "tp"),
            P("ctx", "tp"),
            P("ctx", "tp"),
            P("ctx", None),
            P(None, None, "tp"),
            P("ctx", "tp"),
            P(),
            P(),
            P(),
        ),
        out_specs=(
            P("ctx", "tp"),
            P("ctx", "tp"),
            P("ctx", "tp"),
            P("ctx", None),
            P(None, None, "tp"),
        ),
        check_vma=False,
    )
```

time: 332 us -> 64.1 us (0.19)
  waiting for transfers between devices: 236 us -> 0 us
  Pallas kernels: 0 us -> 55.6 us
  starting transfers between devices: 21.3 us -> 0 us
  between operations: 17.7 us -> 0.66 us
  local copies, waits for them, and re-layouts: 20.7 us -> 7.49 us
  blocking collectives: 13.2 us -> 0 us
  matrix products: 12.5 us -> 0 us
  other arithmetic: 8.96 us -> 0 us
    psum x1 -> x0, waiting for transfers between devices: 207 us -> none  [body(): grad_adapter = lax.psum(adapter_part, 'ctx')]
    pallas_call x0 -> x2, Pallas kernels: none -> 55.6 us  [the longest x1 54.3 us: body(): pl.pallas_call(functools.partial(kernel, side, n_tp), out_shape=(jax.Shap...]
    ppermute x8 -> x0, waiting for transfers between devices: 28.7 us -> none  [passed_along(): return lax.ppermute(array, axis, pairs)]
    ppermute x8 -> x0, starting transfers between devices: 21.3 us -> none  [passed_along(): return lax.ppermute(array, axis, pairs)]
    psum x1 -> x0, blocking collectives: 13.2 us -> none  [body(): grad_input = lax.psum(input_part, 'tp').astype(jnp.bfloat16)]
    dot_general x20 -> x0, matrix products: 12.5 us -> none  [the longest x2 4.73 us: add_values(): jnp.einsum('hqk,khe->qhe', probs_low, split_heads(pair[1]), preferred_ele...]
    cond x8 -> x0, local copies, waits for them, and re-layouts: 5.8 us -> none  [the longest x5 5.21 us: body(): lax.cond(useful, piece_grads, skip_piece, query_gradient)]
    unnamed x39 -> x17, local copies, waits for them, and re-layouts: 8.06 us -> 7.49 us
  transfers between devices with their start and end apart: 9 -> 0, of which waited for: 5 -> 0; matrix products, arithmetic and copies ran while one was open for 3% -> 0% of each run, Pallas kernels for 0% -> 0%
where the time goes in v1:
time: 64.1 us; the launch traced here: 63.7 us
  Pallas kernels  55.6 us (87%)
  local copies, waits for them, and re-layouts  7.49 us (12%)
  between operations  0.66 us (1%)
    pallas_call x1, Pallas kernels, body(): pl.pallas_call(functools.partial(kernel, side, n_tp), out_shape=(jax.Shap...  54.3 us
    unnamed x17, local copies, waits for them, and re-layouts  7.49 us
    pallas_call x1, Pallas kernels, body(): pl.pallas_call(finish, out_shape=(jax.ShapeDtypeStruct((ROWS, COLUMNS), B...  1.33 us

profile of v1, /device:TPU:1, one launch (start us, length us, event | category | flops | bytes accessed | tf_op | source)
XLA Modules:
  0.0 63.7 jit_solution(15112070398737607574)
XLA Ops:
  0.6 0.0 copy-start
  0.6 1.0 %copy-done = bf16[2,128,896]{2,1,0:T(8,128)(2,1)S(1)} copy-done((bf16[2,128,896]{2,1,0:T(8,128)(2,1)S(1)}, bf16[2,128,896]{2,1,0:T(8,128)(2,1)}, u32[]{:S(2)}) %copy-start) | copy-done | bytes 458776
  1.7 0.0 copy-start.1
  1.7 0.9 %copy-done.1 = bf16[128,896]{1,0:T(8,128)(2,1)S(1)} copy-done((bf16[128,896]{1,0:T(8,128)(2,1)S(1)}, bf16[128,896]{1,0:T(8,128)(2,1)}, u32[]{:S(2)}) %copy-start.1) | copy-done | bytes 229400
  2.6 0.0 copy-start.2
  2.6 0.9 %copy-done.2 = bf16[128,896]{1,0:T(8,128)(2,1)S(1)} copy-done((bf16[128,896]{1,0:T(8,128)(2,1)S(1)}, bf16[128,896]{1,0:T(8,128)(2,1)}, u32[]{:S(2)}) %copy-start.2) | copy-done | bytes 229400
  3.5 0.0 copy-start.3
  3.5 0.9 %copy-done.3 = bf16[128,896]{1,0:T(8,128)(2,1)S(1)} copy-done((bf16[128,896]{1,0:T(8,128)(2,1)S(1)}, bf16[128,896]{1,0:T(8,128)(2,1)}, u32[]{:S(2)}) %copy-start.3) | copy-done | bytes 229400
  4.5 0.0 copy-start.4
  4.5 0.9 %copy-done.4 = bf16[128,896]{1,0:T(8,128)(2,1)S(1)} copy-done((bf16[128,896]{1,0:T(8,128)(2,1)S(1)}, bf16[128,896]{1,0:T(8,128)(2,1)}, u32[]{:S(2)}) %copy-start.4) | copy-done | bytes 229400
  5.4 0.0 copy-start.5
  5.4 0.8 %copy-done.5 = bf16[128,128]{1,0:T(8,128)(2,1)S(1)} copy-done((bf16[128,128]{1,0:T(8,128)(2,1)S(1)}, bf16[128,128]{1,0:T(8,128)(2,1)}, u32[]{:S(2)}) %copy-start.5) | copy-done | bytes 32792
  6.2 0.0 copy-start.6
  6.2 0.7 %copy-done.6 = s32[256]{0:T(256)S(1)} copy-done((s32[256]{0:T(256)S(1)}, s32[256]{0:T(256)}, u32[]{:S(2)}) %copy-start.6) | copy-done | bytes 1048
  6.8 0.0 copy-start.7
  6.8 0.7 %copy-done.7 = s32[256]{0:T(256)S(1)} copy-done((s32[256]{0:T(256)S(1)}, s32[256]{0:T(256)}, u32[]{:S(2)}) %copy-start.7) | copy-done | bytes 1048
  7.5 54.3 %shard_map.119 = (bf16[3,2,128,512]{3,2,1,0:T(8,128)(2,1)S(1)}, bf16[128,128]{1,0:T(8,128)(2,1)S(1)}, bf16[2,2,8,16,512]{4,3,2,1,0:T(8,128)(2,1)S(1)}) custom-call(s32[256]{0:T(256)S(1)} %copy-done.6, s32[256]{0:T(256)S(1)} %copy-done.7, bf16[128,896]{1,0:T(8,128)(2,1)S(1)} %copy-done.1, bf16[128,896]{1,0:T(8,128)(2,1)S(1)} %copy-done.2, ...), custom_call_target="tpu_custom_call" | custom-call | tf_op jit(solution)/shard_map/pallas_call | solution.py:408
  61.8 1.3 %shard_map.120 = (bf16[128,896]{1,0:T(8,128)(2,1)}, bf16[128,896]{1,0:T(8,128)(2,1)}, bf16[128,896]{1,0:T(8,128)(2,1)}, f32[2,128,896]{2,1,0:T(8,128)}) custom-call(bf16[3,2,128,512]{3,2,1,0:T(8,128)(2,1)S(1)} %get-tuple-element.12.out_ref, bf16[2,2,128,512]{3,2,1,0:T(8,128)(2,1)S(1)} %bitcast.1), custom_call_target="tpu_custom_call" | custom-call | tf_op jit(solution)/shard_map/pallas_call | solution.py:454
  63.1 0.6 copy.14
Async XLA Ops:
  0.6 1.0 %copy-start = (bf16[2,128,896]{2,1,0:T(8,128)(2,1)S(1)}, bf16[2,128,896]{2,1,0:T(8,128)(2,1)}, u32[]{:S(2)}) copy-start(bf16[2,128,896]{2,1,0:T(8,128)(2,1)} %w_hbm.1) | copy-start | bytes 1376260
  1.7 0.9 %copy-start.1 = (bf16[128,896]{1,0:T(8,128)(2,1)S(1)}, bf16[128,896]{1,0:T(8,128)(2,1)}, u32[]{:S(2)}) copy-start(bf16[128,896]{1,0:T(8,128)(2,1)} %q_hbm.1) | copy-start | bytes 688132
  2.6 0.9 %copy-start.2 = (bf16[128,896]{1,0:T(8,128)(2,1)S(1)}, bf16[128,896]{1,0:T(8,128)(2,1)}, u32[]{:S(2)}) copy-start(bf16[128,896]{1,0:T(8,128)(2,1)} %k_hbm.1) | copy-start | bytes 688132
  3.5 0.9 %copy-start.3 = (bf16[128,896]{1,0:T(8,128)(2,1)S(1)}, bf16[128,896]{1,0:T(8,128)(2,1)}, u32[]{:S(2)}) copy-start(bf16[128,896]{1,0:T(8,128)(2,1)} %v_hbm.1) | copy-start | bytes 688132
  4.5 0.9 %copy-start.4 = (bf16[128,896]{1,0:T(8,128)(2,1)S(1)}, bf16[128,896]{1,0:T(8,128)(2,1)}, u32[]{:S(2)}) copy-start(bf16[128,896]{1,0:T(8,128)(2,1)} %g_hbm.1) | copy-start | bytes 688132
  5.4 0.8 %copy-start.5 = (bf16[128,128]{1,0:T(8,128)(2,1)S(1)}, bf16[128,128]{1,0:T(8,128)(2,1)}, u32[]{:S(2)}) copy-start(bf16[128,128]{1,0:T(8,128)(2,1)} %a_hbm.1) | copy-start | bytes 98308
  6.2 0.7 %copy-start.6 = (s32[256]{0:T(256)S(1)}, s32[256]{0:T(256)}, u32[]{:S(2)}) copy-start(s32[256]{0:T(256)} %slot_ref.1) | copy-start | bytes 3076
  6.8 0.7 %copy-start.7 = (s32[256]{0:T(256)S(1)}, s32[256]{0:T(256)}, u32[]{:S(2)}) copy-start(s32[256]{0:T(256)} %first_ref.1) | copy-start | bytes 3076

commit v2 on v1

--- a/solution.py
+++ b/solution.py
@@ -28,8 +28,9 @@
 S_INPUT = 8
 S_ADAPTER = 9
 S_NEXT = 11
-S_BACK = 13
-S_ALONG = 15
+S_BACK = 15
+S_PAST = 19
+S_ALONG = 21
 MESH = pl.DeviceIdType.MESH
 F32 = jnp.float32
 BF16 = jnp.bfloat16
@@ -58,7 +59,7 @@
     side, n_tp,
     slot_ref, first_ref, q_hbm, k_hbm, v_hbm, a_hbm, w_hbm, g_hbm,
     out_ref, gi_ref, ga_ref,
-    raw, act, weight, weight_pad, packed, sibling, act_sib, act_sorted,
+    raw, act, weight, weight_pad, packed, sibling, act_sib, act_past, act_window,
     window_kv, sorted_qg, probs, probs_low, back_send, back_recv, own_kv,
     grads, sib_send, outs, gi_send, gi_sib, gi_along,
     part, scattered, crossed, gathered,
@@ -101,7 +102,9 @@
     def greet(ctx, x):
         pl.semaphore_signal(barrier, inc=1, device_id=(ctx, x), device_id_type=MESH)
 
-    for device in (other, after, before):
+    after_other = after + 1 - 2 * core
+    before_other = before + 1 - 2 * core
+    for device in (other, after, after_other, before, before_other):
         greet(device, tp)
 
     def greet_side(step, carry):
@@ -121,8 +124,10 @@
         slot_ref[2 * me] - 4 * chip, slot_ref[2 * me + 1] - 4 * chip,
         slot_ref[2 * other] - 4 * chip, slot_ref[2 * other + 1] - 4 * chip,
     ]
-
-    def in_order(own, sib):
+    past = lax.rem(chip + chips - 1, chips)
+    past_places = [slot_ref[4 * past + j] - 4 * past for j in range(4)]
+
+    def in_order(own, sib, places=places):
         slots = [own[:STRETCH], own[STRETCH:], sib[:STRETCH], sib[STRETCH:]]
         result = []
         for i in range(4):
@@ -150,12 +155,18 @@
 
     loads[0].wait()
     pack(KEY, padded(raw[KEY]))
-    pl.semaphore_wait(barrier, 3 + 2 * (side - 1) + n_tp - 1)
+    loads[1].wait()
+    pl.semaphore_wait(barrier, 5 + 2 * (side - 1) + n_tp - 1)
     sib_key = to_sibling(KEY, S_KEY)
     sib_key.start()
-    loads[1].wait()
     sib_act = remote(act, act_sib, S_ACT, other)
     sib_act.start()
+    past_acts = [
+        remote(act, act_past.at[core], S_PAST, after),
+        remote(act, act_past.at[core], S_PAST + 1, after_other),
+    ]
+    for copy in past_acts:
+        copy.start()
     loads[2].wait()
     for i in range(2):
         wide = padded(weight[i])
@@ -179,20 +190,23 @@
         for i, values in enumerate(in_order(packed[kind, core], sibling[kind])):
             window_kv[kind, GROUP_ROWS + i * STRETCH:GROUP_ROWS + (i + 1) * STRETCH] = values
 
-    def to_next(kind):
+    def to_next(kind, head):
+        lanes = pl.ds(head * PAD, PAD)
         return remote(
-            window_kv.at[kind, pl.ds(GROUP_ROWS + STRETCH, SENT)],
-            window_kv.at[kind, pl.ds(STRETCH, SENT)], S_NEXT + kind, after,
+            window_kv.at[kind, pl.ds(GROUP_ROWS + STRETCH, SENT), lanes],
+            window_kv.at[kind, pl.ds(STRETCH, SENT), lanes], S_NEXT + 2 * head + kind, after,
         )
 
+    next_kv = {}
     sib_key.wait_recv()
     spread(KEY)
-    next_key = to_next(KEY)
-    next_key.start()
+    next_kv[KEY, 0] = to_next(KEY, 0)
+    next_kv[KEY, 0].start()
     sib_value.wait_recv()
     spread(VALUE)
-    next_value = to_next(VALUE)
-    next_value.start()
+    for kind, head in ((VALUE, 0), (KEY, 1), (VALUE, 1)):
+        next_kv[kind, head] = to_next(kind, head)
+        next_kv[kind, head].start()
 
     loads[4].wait()
     adapt(QUERY, 0)
@@ -205,7 +219,13 @@
 
     sib_act.wait_recv()
     for i, values in enumerate(in_order(act[...], act_sib[...])):
-        act_sorted[i * STRETCH:(i + 1) * STRETCH] = values
+        act_window[GROUP_ROWS + i * STRETCH:GROUP_ROWS + (i + 1) * STRETCH] = values
+    for copy in past_acts:
+        copy.wait_recv()
+    act_window[:STRETCH] = jnp.zeros((STRETCH, RANK), BF16)
+    for i, values in enumerate(in_order(act_past[0], act_past[1], past_places)):
+        if i:
+            act_window[i * STRETCH:(i + 1) * STRETCH] = values
     for kind, copy in ((QUERY, sib_query), (GRAD, sib_grad)):
         copy.wait_recv()
         for i, values in enumerate(in_order(packed[kind, core], sibling[kind])):
@@ -219,9 +239,43 @@
         lowest = jnp.where(query_place >= i * STRETCH, start, lowest)
     visible = (key_place >= lowest) & (key_place <= query_place + GROUP_ROWS)
 
-    next_key.wait_recv()
+    def along_sem(unit, stage, step):
+        return S_ALONG + (unit * 3 + stage) * side + step
+
+    position = [(y, z), (z, y)]
+
+    def scatter(unit, step):
+        target = lax.rem(position[unit][0] + step, side)
+        return remote(
+            part.at[unit, target], scattered.at[unit, step], along_sem(unit, 0, step), along(unit, step)
+        )
+
+    def cross(unit, step):
+        block = crossed.at[unit, position[unit][1]]
+        return remote(block, block, along_sem(unit, 1, step), along(1 - unit, step))
+
+    def gather(unit, step):
+        block = gathered.at[unit, core, position[unit][0]]
+        return remote(block, block, along_sem(unit, 2, step), along(unit, step))
+
+    def each(make, unit, method):
+        def run(step, carry):
+            getattr(make(unit, step), method)()
+            return carry
+
+        lax.fori_loop(1, side, run, 0)
+
+    def back(kind, head):
+        lanes = pl.ds(head * PAD, PAD)
+        return remote(
+            back_send.at[kind, :, lanes], back_recv.at[kind, :, lanes],
+            S_BACK + 2 * head + kind, before,
+        )
+
+    backs = {}
     for head in range(2):
         lanes = slice(head * PAD, (head + 1) * PAD)
+        next_kv[KEY, head].wait_recv()
         scores = dot(window_kv[KEY, :, lanes], sorted_qg[0, :, lanes], (1, 1)) * SCALE
         scores = jnp.where(visible, scores, FILL)
         peak = jnp.max(scores, axis=0, keepdims=True)
@@ -231,72 +285,42 @@
         low = share.astype(BF16)
         probs_low[head] = low
         terms = dot(low, sorted_qg[1, :, lanes], (1, 0))
-        back_send[VALUE, :, lanes] = terms[STRETCH:GROUP_ROWS].astype(BF16)
         own_kv[VALUE, :, lanes] = terms[GROUP_ROWS:]
-    back_value = remote(back_send.at[VALUE], back_recv.at[VALUE], S_BACK + VALUE, before)
-    back_value.start()
-
-    next_value.wait_recv()
-    for head in range(2):
-        lanes = slice(head * PAD, (head + 1) * PAD)
+        terms = terms.astype(BF16)
+        back_send[VALUE, :, lanes] = terms[STRETCH:GROUP_ROWS]
+        backs[VALUE, head] = back(VALUE, head)
+        backs[VALUE, head].start()
+        adapter = dot(act_window[...], terms, (0, 0)).astype(BF16)
+        for j in range(side):
+            part[head, j, 1] = adapter[j * rows:(j + 1) * rows]
+
+        next_kv[VALUE, head].wait_recv()
         grad_probs = dot(window_kv[VALUE, :, lanes], sorted_qg[1, :, lanes], (1, 1))
         row_dot = jnp.sum(probs_low[head].astype(F32) * grad_probs, axis=0, keepdims=True)
         grad_scores = (probs[head] * (grad_probs - row_dot)).astype(BF16)
+        summed = (dot(grad_scores, window_kv[KEY, :, lanes], (0, 0)) * SCALE).astype(BF16)
+        grads[0, :, lanes] = summed
+        adapter = dot(act_window[GROUP_ROWS:], summed, (0, 0)).astype(BF16)
+        for j in range(side):
+            part[head, j, 0] = adapter[j * rows:(j + 1) * rows]
+        each(scatter, head, "start")
         terms = dot(grad_scores, sorted_qg[0, :, lanes], (1, 0)) * SCALE
         back_send[KEY, :, lanes] = terms[STRETCH:GROUP_ROWS].astype(BF16)
         own_kv[KEY, :, lanes] = terms[GROUP_ROWS:]
-        summed = dot(grad_scores, window_kv[KEY, :, lanes], (0, 0)) * SCALE
-        grads[0, :, lanes] = summed.astype(BF16)
-    back_key = remote(back_send.at[KEY], back_recv.at[KEY], S_BACK + KEY, before)
-    back_key.start()
-
-    def along_sem(t, stage, step):
-        return S_ALONG + (t * 3 + stage) * side + step
-
-    position = [(y, z), (z, y)]
-
-    def scatter(t, step):
-        target = lax.rem(position[t][0] + step, side)
-        return remote(part.at[t, target], scattered.at[t, step], along_sem(t, 0, step), along(t, step))
-
-    def cross(t, step):
-        mine = position[t][1]
-        return remote(crossed.at[t, mine], crossed.at[t, mine], along_sem(t, 1, step), along(1 - t, step))
-
-    def gather(t, step):
-        mine = position[t][0]
-        return remote(
-            gathered.at[t, core, mine], gathered.at[t, core, mine], along_sem(t, 2, step), along(t, step)
-        )
-
-    def each(make, t, method):
-        def run(step, carry):
-            getattr(make(t, step), method)()
-            return carry
-
-        lax.fori_loop(1, side, run, 0)
-
-    def adapter_terms(t, values):
-        terms = dot(act_sorted[...], values, (0, 0)).astype(BF16)
-        for j in range(side):
-            part[t, j] = terms[j * rows:(j + 1) * rows]
-        each(scatter, t, "start")
-
-    def input_terms(t, values):
-        return dot(values, weight_pad[t, core], (1, 1))
-
-    def hand_out(t, slots):
-        outs[t, core, :STRETCH] = slots[0]
-        outs[t, core, STRETCH:] = slots[1]
-        sib_send[t, :STRETCH] = slots[2]
-        sib_send[t, STRETCH:] = slots[3]
-        copy = remote(sib_send.at[t], outs.at[t, core], S_OUT + t, other)
+        backs[KEY, head] = back(KEY, head)
+        backs[KEY, head].start()
+
+    def input_terms(i, values):
+        return dot(values, weight_pad[i, core], (1, 1))
+
+    def hand_out(i, slots):
+        outs[i, core, :STRETCH] = slots[0]
+        outs[i, core, STRETCH:] = slots[1]
+        sib_send[i, :STRETCH] = slots[2]
+        sib_send[i, STRETCH:] = slots[3]
+        copy = remote(sib_send.at[i], outs.at[i, core], S_OUT + i, other)
         copy.start()
         return copy
-
-    adapter_terms(0, grads[0])
-    input_part = input_terms(0, grads[0])
-    out_query = hand_out(0, to_slots(grads[0]))
 
     def add_back(kind):
         mine = own_kv[kind]
@@ -304,27 +328,42 @@
             [mine[:STRETCH], mine[STRETCH:] + back_recv[kind].astype(F32)], axis=0
         ).astype(BF16)
 
-    back_value.wait_recv()
+    def go_across(unit):
+        each(scatter, unit, "wait_recv")
+        total = part[unit, position[unit][0]].astype(F32)
+        for step in range(1, side):
+            total = total + scattered[unit, step].astype(F32)
+        crossed[unit, position[unit][1]] = total.astype(BF16)
+        each(cross, unit, "start")
+
+    def go_around(unit):
+        each(cross, unit, "wait_recv")
+        total = crossed[unit, 0].astype(F32)
+        for step in range(1, side):
+            total = total + crossed[unit, step].astype(F32)
+        gathered[unit, core, position[unit][0]] = total.astype(BF16)
+        each(gather, unit, "start")
+
+    input_part = input_terms(0, grads[0])
+    out_query = hand_out(0, to_slots(grads[0]))
+    go_across(0)
+
+    for head in range(2):
+        backs[VALUE, head].wait_recv()
     grads[1] = add_back(VALUE)
-    adapter_terms(1, grads[1])
     input_slots = to_slots(input_part + input_terms(1, grads[1]))
     gi_send[:STRETCH] = input_slots[2]
     gi_send[STRETCH:] = input_slots[3]
     sib_input = remote(gi_send, gi_sib, S_INPUT, other)
     sib_input.start()
+    gi_along[tp, :STRETCH] = input_slots[0]
+    gi_along[tp, STRETCH:] = input_slots[1]
     out_value = hand_out(2, to_slots(grads[1]))
 
-    for t in range(2):
-        each(scatter, t, "wait_recv")
-        total = part[t, position[t][0]].astype(F32)
-        for step in range(1, side):
-            total = total + scattered[t, step].astype(F32)
-        crossed[t, position[t][1]] = total.astype(BF16)
-        each(cross, t, "start")
+    go_across(1)
 
     sib_input.wait_recv()
-    gi_along[tp, :STRETCH] = input_slots[0] + gi_sib[:STRETCH]
-    gi_along[tp, STRETCH:] = input_slots[1] + gi_sib[STRETCH:]
+    gi_along[tp] = gi_along[tp] + gi_sib[...]
 
     def tp_copy(step):
         return remote(
@@ -339,55 +378,56 @@
         lax.fori_loop(1, n_tp, run, 0)
 
     each_tp("start")
-
-    for t in range(2):
-        each(cross, t, "wait_recv")
-        total = crossed[t, 0].astype(F32)
-        for step in range(1, side):
-            total = total + crossed[t, step].astype(F32)
-        gathered[t, core, position[t][0]] = total.astype(BF16)
-        each(gather, t, "start")
-
-    back_key.wait_recv()
+    for head in range(2):
+        backs[KEY, head].wait_recv()
     out_key = hand_out(1, to_slots(add_back(KEY)))
 
+    go_around(0)
     each_tp("wait_recv")
     total = gi_along[0]
     for x in range(1, n_tp):
         total = total + gi_along[x]
     gi_ref[...] = total.astype(BF16)
-
-    sib_adapter = []
-    for t in range(2):
-        each(gather, t, "wait_recv")
-        copy = remote(gathered.at[t, core], gathered.at[t, core], S_ADAPTER + t, other)
-        copy.start()
-        sib_adapter.append(copy)
+    go_around(1)
 
     for copy in (out_query, out_value, out_key):
         copy.wait_recv()
     out_ref[...] = outs[...]
-    for copy in sib_adapter:
-        copy.wait_recv()
-    ga_ref[...] = gathered[...]
+
+    sib_adapter = []
+    for unit in range(2):
+        each(gather, unit, "wait_recv")
+        block = gathered.at[unit, core]
+        copy = remote(block, block, S_ADAPTER + unit, other)
+        copy.start()
+        sib_adapter.append(copy)
 
     for copy in (
-        sib_key, sib_act, sib_value, next_key, next_value, sib_query, sib_grad, back_value, back_key,
-        out_query, out_value, out_key, sib_input, *sib_adapter,
+        sib_key, sib_act, sib_value, sib_query, sib_grad, *past_acts, *next_kv.values(),
+        *backs.values(), out_query, out_value, out_key, sib_input,
     ):
         copy.wait_send()
-    for t in range(2):
-        each(scatter, t, "wait_send")
-        each(cross, t, "wait_send")
-        each(gather, t, "wait_send")
+    for unit in range(2):
+        each(scatter, unit, "wait_send")
+        each(cross, unit, "wait_send")
+        each(gather, unit, "wait_send")
     each_tp("wait_send")
-
-
-def finish(out_ref, ga_ref, q_ref, k_ref, v_ref, adapter_ref):
+    for unit in range(2):
+        sib_adapter[unit].wait_recv()
+        ga_ref[unit] = gathered[unit]
+        sib_adapter[unit].wait_send()
+
+
+def finish(out_ref, gi_ref, ga_ref, q_ref, k_ref, v_ref, input_ref, adapter_ref):
+    input_ref[...] = gi_ref[...]
     for i, ref in enumerate((q_ref, k_ref, v_ref)):
         ref[...] = unpadded([out_ref[i, 0], out_ref[i, 1]])
     for i in range(2):
-        adapter_ref[i] = unpadded([ga_ref[i, 0].astype(F32), ga_ref[i, 1].astype(F32)])
+        heads = [
+            ga_ref[unit, pair, :, i].reshape(RANK, PAD)[:, :HEAD].astype(F32)
+            for pair in range(2) for unit in range(2)
+        ]
+        adapter_ref[i] = jnp.concatenate(heads, axis=1)
 
 
 def body(
@@ -398,7 +438,7 @@
     side = math.isqrt(lax.axis_size("ctx") // 2)
     rows = RANK // side
     copies = S_ALONG + 6 * side + n_tp
-    anywhere = pl.BlockSpec(memory_space=pl.ANY)
+    anywhere = pl.BlockSpec(memory_space=pltpu.HBM)
     vmem = pl.BlockSpec(memory_space=pltpu.VMEM)
     smem = pl.BlockSpec(memory_space=pltpu.SMEM)
 
@@ -410,7 +450,7 @@
         out_shape=(
             jax.ShapeDtypeStruct((3, 2, ROWS, PAIR), BF16),
             jax.ShapeDtypeStruct((ROWS, RANK), BF16),
-            jax.ShapeDtypeStruct((2, 2, side, rows, PAIR), BF16),
+            jax.ShapeDtypeStruct((2, 2, side, 2, rows, PAD), BF16),
         ),
         in_specs=[smem, smem] + [anywhere] * 6,
         out_specs=(vmem, vmem, vmem),
@@ -422,7 +462,8 @@
             block(4, 2, ROWS, PAIR),
             block(4, ROWS, PAIR),
             block(ROWS, RANK),
-            block(GROUP_ROWS, RANK),
+            block(2, ROWS, RANK),
+            block(WINDOW, RANK),
             block(2, WINDOW, PAIR),
             block(2, GROUP_ROWS, PAIR),
             block(2, WINDOW, GROUP_ROWS, dtype=F32),
@@ -436,34 +477,34 @@
             block(ROWS, RANK, dtype=F32),
             block(ROWS, RANK, dtype=F32),
             block(n_tp, ROWS, RANK, dtype=F32),
-            block(2, side, rows, PAIR),
-            block(2, side, rows, PAIR),
-            block(2, side, rows, PAIR),
-            block(2, 2, side, rows, PAIR),
+            block(2, side, 2, rows, PAD),
+            block(2, side, 2, rows, PAD),
+            block(2, side, 2, rows, PAD),
+            block(2, 2, side, 2, rows, PAD),
             pltpu.SemaphoreType.DMA((6,)),
             pltpu.SemaphoreType.DMA((copies,)),
             pltpu.SemaphoreType.DMA((copies,)),
         ],
         compiler_params=pltpu.CompilerParams(
-            collective_id=0, has_side_effects=True, vmem_limit_bytes=48 * 2**20
+            collective_id=0, has_side_effects=True, vmem_limit_bytes=56 * 2**20
         ),
     )(
         slot_stretch, doc_first, query_base, key_base, value_base, adapter_activation,
         adapter_up_weight, output_grad,
     )
-    grad_query, grad_key, grad_value, grad_adapter = pl.pallas_call(
+    return pl.pallas_call(
         finish,
         out_shape=(
             jax.ShapeDtypeStruct((ROWS, COLUMNS), BF16),
             jax.ShapeDtypeStruct((ROWS, COLUMNS), BF16),
             jax.ShapeDtypeStruct((ROWS, COLUMNS), BF16),
+            jax.ShapeDtypeStruct((ROWS, RANK), BF16),
             jax.ShapeDtypeStruct((2, RANK, COLUMNS), F32),
         ),
-        in_specs=[vmem, vmem],
-        out_specs=(vmem,) * 4,
-        compiler_params=pltpu.CompilerParams(vmem_limit_bytes=48 * 2**20),
-    )(outs, adapter.reshape(2, 2, RANK, PAIR))
-    return grad_query, grad_key, grad_value, grad_input, grad_adapter
+        in_specs=[vmem] * 3,
+        out_specs=(vmem,) * 5,
+        compiler_params=pltpu.CompilerParams(vmem_limit_bytes=56 * 2**20),
+    )(outs, grad_input, adapter)
 
 
 def solution(mesh):

time: 64.1 us -> 55.6 us (0.87)
  local copies, waits for them, and re-layouts: 7.49 us -> 0 us
  Pallas kernels: 55.6 us -> 54.7 us
    unnamed x17 -> x0, local copies, waits for them, and re-layouts: 7.49 us -> none
    pallas_call x1, Pallas kernels: 54.3 us -> 52.1 us  [body(): pl.pallas_call(functools.partial(kernel, side, n_tp), out_shape=(jax.Shap...]
    pallas_call x1, Pallas kernels: 1.33 us -> 2.63 us  [body(): pl.pallas_call(finish, out_shape=(jax.ShapeDtypeStruct((ROWS, COLUMNS), B...]
where the time goes in v2:
time: 55.6 us; the launch traced here: 55.4 us
  Pallas kernels  54.7 us (98%)
  between operations  0.64 us (1%)
    pallas_call x1, Pallas kernels, body(): pl.pallas_call(functools.partial(kernel, side, n_tp), out_shape=(jax.Shap...  52.1 us
    pallas_call x1, Pallas kernels, body(): pl.pallas_call(finish, out_shape=(jax.ShapeDtypeStruct((ROWS, COLUMNS), B...  2.63 us

profile of v2, /device:TPU:1, one launch (start us, length us, event | category | flops | bytes accessed | tf_op | source)
XLA Modules:
  0.0 55.4 jit_solution(13842364687330067273)
XLA Ops:
  0.6 52.1 %shard_map.119 = (bf16[3,2,128,512]{3,2,1,0:T(8,128)(2,1)}, bf16[128,128]{1,0:T(8,128)(2,1)}, bf16[2,2,8,2,16,256]{5,4,3,2,1,0:T(8,128)(2,1)}) custom-call(s32[256]{0:T(256)} %slot_ref.1, s32[256]{0:T(256)} %first_ref.1, bf16[128,896]{1,0:T(8,128)(2,1)} %q_hbm.1, bf16[128,896]{1,0:T(8,128)(2,1)} %k_hbm.1, bf16[128,896]{1,0:T(8,128)(2,1)} %v_hbm.1, ...), custom_call_target="tpu_custom_call" | custom-call | tf_op jit(solution)/shard_map/pallas_call | solution.py:448
  52.7 2.6 %shard_map.120 = (bf16[128,896]{1,0:T(8,128)(2,1)}, bf16[128,896]{1,0:T(8,128)(2,1)}, bf16[128,896]{1,0:T(8,128)(2,1)}, bf16[128,128]{1,0:T(8,128)(2,1)}, f32[2,128,896]{2,1,0:T(8,128)}) custom-call(bf16[3,2,128,512]{3,2,1,0:T(8,128)(2,1)} %get-tuple-element.8.out_ref, bf16[128,128]{1,0:T(8,128)(2,1)} %get-tuple-element.9.gi_ref, ...), custom_call_target="tpu_custom_call" | custom-call | tf_op jit(solution)/shard_map/pallas_call | solution.py:495

commit v3 on v2

--- a/solution.py
+++ b/solution.py
@@ -30,7 +30,8 @@
 S_NEXT = 11
 S_BACK = 15
 S_PAST = 19
-S_ALONG = 21
+S_FIRST = 21
+S_ALONG = 22
 MESH = pl.DeviceIdType.MESH
 F32 = jnp.float32
 BF16 = jnp.bfloat16
@@ -58,12 +59,12 @@
 def kernel(
     side, n_tp,
     slot_ref, first_ref, q_hbm, k_hbm, v_hbm, a_hbm, w_hbm, g_hbm,
-    out_ref, gi_ref, ga_ref,
-    raw, act, weight, weight_pad, packed, sibling, act_sib, act_past, act_window,
+    out_hbm, gi_hbm, ga_hbm,
+    raw, act, weight, weight_pad, packed, sibling, act_sib, act_past, act_window, key_past,
     window_kv, sorted_qg, probs, probs_low, back_send, back_recv, own_kv,
     grads, sib_send, outs, gi_send, gi_sib, gi_along,
-    part, scattered, crossed, gathered,
-    load_sem, send_sem, recv_sem,
+    part, scattered, crossed, gathered, gi_out,
+    load_sem, store_sem, send_sem, recv_sem,
 ):
     me = lax.axis_index("ctx")
     tp = lax.axis_index("tp")
@@ -94,31 +95,25 @@
             (q_hbm, raw.at[QUERY]), (g_hbm, raw.at[GRAD]),
         ])
     ]
-    for load in loads:
-        load.start()
+    loads[0].start()
 
     barrier = pltpu.get_barrier_semaphore()
 
     def greet(ctx, x):
         pl.semaphore_signal(barrier, inc=1, device_id=(ctx, x), device_id_type=MESH)
 
+    steps = [side // 2 + (i // 2) * (1 - 2 * (i % 2)) for i in range(1, side)]
+    for step in steps:
+        greet(along(0, step), tp)
+        greet(along(1, step), tp)
+    for step in range(1, n_tp):
+        greet(me, lax.rem(tp + step, n_tp))
     after_other = after + 1 - 2 * core
     before_other = before + 1 - 2 * core
-    for device in (other, after, after_other, before, before_other):
+    for device in (after, after_other, before, before_other, other):
         greet(device, tp)
-
-    def greet_side(step, carry):
-        greet(along(0, step), tp)
-        greet(along(1, step), tp)
-        return carry
-
-    lax.fori_loop(1, side, greet_side, 0)
-
-    def greet_tp(step, carry):
-        greet(me, lax.rem(tp + step, n_tp))
-        return carry
-
-    lax.fori_loop(1, n_tp, greet_tp, 0)
+    for load in loads[1:]:
+        load.start()
 
     places = [
         slot_ref[2 * me] - 4 * chip, slot_ref[2 * me + 1] - 4 * chip,
@@ -161,12 +156,15 @@
     sib_key.start()
     sib_act = remote(act, act_sib, S_ACT, other)
     sib_act.start()
-    past_acts = [
-        remote(act, act_past.at[core], S_PAST, after),
-        remote(act, act_past.at[core], S_PAST + 1, after_other),
+    first = pl.ds(0, PAD)
+    next_first = [
+        remote(packed.at[KEY, core, :, first], key_past.at[core], S_NEXT, after),
+        remote(packed.at[KEY, 1 - core, :, first], key_past.at[core], S_FIRST, after_other),
     ]
-    for copy in past_acts:
+    for copy in next_first:
         copy.start()
+    next_act = remote(act, act_past.at[core], S_PAST, after)
+    next_act.start()
     loads[2].wait()
     for i in range(2):
         wide = padded(weight[i])
@@ -200,8 +198,6 @@
     next_kv = {}
     sib_key.wait_recv()
     spread(KEY)
-    next_kv[KEY, 0] = to_next(KEY, 0)
-    next_kv[KEY, 0].start()
     sib_value.wait_recv()
     spread(VALUE)
     for kind, head in ((VALUE, 0), (KEY, 1), (VALUE, 1)):
@@ -220,16 +216,13 @@
     sib_act.wait_recv()
     for i, values in enumerate(in_order(act[...], act_sib[...])):
         act_window[GROUP_ROWS + i * STRETCH:GROUP_ROWS + (i + 1) * STRETCH] = values
-    for copy in past_acts:
-        copy.wait_recv()
-    act_window[:STRETCH] = jnp.zeros((STRETCH, RANK), BF16)
-    for i, values in enumerate(in_order(act_past[0], act_past[1], past_places)):
-        if i:
-            act_window[i * STRETCH:(i + 1) * STRETCH] = values
     for kind, copy in ((QUERY, sib_query), (GRAD, sib_grad)):
         copy.wait_recv()
         for i, values in enumerate(in_order(packed[kind, core], sibling[kind])):
             sorted_qg[kind - QUERY, i * STRETCH:(i + 1) * STRETCH] = values
+    next_act.wait_recv()
+    pass_act = remote(act_past.at[core], act_past.at[core], S_PAST + 1, other)
+    pass_act.start()
 
     key_place = lax.broadcasted_iota(jnp.int32, (WINDOW, GROUP_ROWS), 0)
     query_place = lax.broadcasted_iota(jnp.int32, (1, GROUP_ROWS), 1)
@@ -259,6 +252,11 @@
         return remote(block, block, along_sem(unit, 2, step), along(unit, step))
 
     def each(make, unit, method):
+        if method == "start":
+            for step in steps:
+                make(unit, step).start()
+            return
+
         def run(step, carry):
             getattr(make(unit, step), method)()
             return carry
@@ -275,7 +273,14 @@
     backs = {}
     for head in range(2):
         lanes = slice(head * PAD, (head + 1) * PAD)
-        next_kv[KEY, head].wait_recv()
+        if head:
+            next_kv[KEY, head].wait_recv()
+        else:
+            for copy in next_first:
+                copy.wait_recv()
+            for i, values in enumerate(in_order(key_past[0], key_past[1], past_places)):
+                if i:
+                    window_kv[KEY, i * STRETCH:(i + 1) * STRETCH, lanes] = values
         scores = dot(window_kv[KEY, :, lanes], sorted_qg[0, :, lanes], (1, 1)) * SCALE
         scores = jnp.where(visible, scores, FILL)
         peak = jnp.max(scores, axis=0, keepdims=True)
@@ -290,6 +295,12 @@
         back_send[VALUE, :, lanes] = terms[STRETCH:GROUP_ROWS]
         backs[VALUE, head] = back(VALUE, head)
         backs[VALUE, head].start()
+        if not head:
+            pass_act.wait_recv()
+            act_window[:STRETCH] = jnp.zeros((STRETCH, RANK), BF16)
+            for i, values in enumerate(in_order(act_past[0], act_past[1], past_places)):
+                if i:
+                    act_window[i * STRETCH:(i + 1) * STRETCH] = values
         adapter = dot(act_window[...], terms, (0, 0)).astype(BF16)
         for j in range(side):
             part[head, j, 1] = adapter[j * rows:(j + 1) * rows]
@@ -387,12 +398,15 @@
     total = gi_along[0]
     for x in range(1, n_tp):
         total = total + gi_along[x]
-    gi_ref[...] = total.astype(BF16)
+    gi_out[...] = total.astype(BF16)
+    stores = [pltpu.make_async_copy(gi_out, gi_hbm, store_sem.at[0])]
+    stores[0].start()
     go_around(1)
 
     for copy in (out_query, out_value, out_key):
         copy.wait_recv()
-    out_ref[...] = outs[...]
+    stores.append(pltpu.make_async_copy(outs, out_hbm, store_sem.at[1]))
+    stores[1].start()
 
     sib_adapter = []
     for unit in range(2):
@@ -403,7 +417,7 @@
         sib_adapter.append(copy)
 
     for copy in (
-        sib_key, sib_act, sib_value, sib_query, sib_grad, *past_acts, *next_kv.values(),
+        sib_key, sib_act, sib_value, sib_query, sib_grad, *next_first, next_act, pass_act, *next_kv.values(),
         *backs.values(), out_query, out_value, out_key, sib_input,
     ):
         copy.wait_send()
@@ -414,20 +428,43 @@
     each_tp("wait_send")
     for unit in range(2):
         sib_adapter[unit].wait_recv()
-        ga_ref[unit] = gathered[unit]
+        stores.append(pltpu.make_async_copy(gathered.at[unit], ga_hbm.at[unit], store_sem.at[2 + unit]))
+        stores[2 + unit].start()
         sib_adapter[unit].wait_send()
-
-
-def finish(out_ref, gi_ref, ga_ref, q_ref, k_ref, v_ref, input_ref, adapter_ref):
-    input_ref[...] = gi_ref[...]
-    for i, ref in enumerate((q_ref, k_ref, v_ref)):
-        ref[...] = unpadded([out_ref[i, 0], out_ref[i, 1]])
+    for store in stores:
+        store.wait()
+
+
+def finish(
+    out_hbm, gi_hbm, ga_hbm, q_hbm, k_hbm, v_hbm, input_hbm, adapter_hbm,
+    outs, gathered, wide, adapter, load_sem, store_sem,
+):
+    loads = [pltpu.make_async_copy(out_hbm.at[i], outs.at[i], load_sem.at[i]) for i in range(3)]
+    loads += [pltpu.make_async_copy(ga_hbm.at[i], gathered.at[i], load_sem.at[3 + i]) for i in range(2)]
+    for load in loads:
+        load.start()
+    stores = [
+        pltpu.make_async_copy(wide.at[i], hbm, store_sem.at[i])
+        for i, hbm in enumerate((q_hbm, k_hbm, v_hbm))
+    ]
+    stores += [pltpu.make_async_copy(adapter.at[i], adapter_hbm.at[i], store_sem.at[3 + i]) for i in range(2)]
+    stores += [pltpu.make_async_copy(gi_hbm, input_hbm, store_sem.at[5])]
+    stores[5].start()
+    for i in range(3):
+        loads[i].wait()
+        wide[i] = unpadded([outs[i, 0], outs[i, 1]])
+        stores[i].start()
+    loads[3].wait()
+    loads[4].wait()
     for i in range(2):
         heads = [
-            ga_ref[unit, pair, :, i].reshape(RANK, PAD)[:, :HEAD].astype(F32)
+            gathered[unit, pair, :, i].reshape(RANK, PAD)[:, :HEAD].astype(F32)
             for pair in range(2) for unit in range(2)
         ]
-        adapter_ref[i] = jnp.concatenate(heads, axis=1)
+        adapter[i] = jnp.concatenate(heads, axis=1)
+        stores[3 + i].start()
+    for store in stores:
+        store.wait()
 
 
 def body(
@@ -439,7 +476,6 @@
     rows = RANK // side
     copies = S_ALONG + 6 * side + n_tp
     anywhere = pl.BlockSpec(memory_space=pltpu.HBM)
-    vmem = pl.BlockSpec(memory_space=pltpu.VMEM)
     smem = pl.BlockSpec(memory_space=pltpu.SMEM)
 
     def block(*shape, dtype=BF16):
@@ -453,7 +489,7 @@
             jax.ShapeDtypeStruct((2, 2, side, 2, rows, PAD), BF16),
         ),
         in_specs=[smem, smem] + [anywhere] * 6,
-        out_specs=(vmem, vmem, vmem),
+        out_specs=(anywhere,) * 3,
         scratch_shapes=[
             block(4, ROWS, COLUMNS),
             block(ROWS, RANK),
@@ -464,6 +500,7 @@
             block(ROWS, RANK),
             block(2, ROWS, RANK),
             block(WINDOW, RANK),
+            block(2, ROWS, PAD),
             block(2, WINDOW, PAIR),
             block(2, GROUP_ROWS, PAIR),
             block(2, WINDOW, GROUP_ROWS, dtype=F32),
@@ -481,7 +518,9 @@
             block(2, side, 2, rows, PAD),
             block(2, side, 2, rows, PAD),
             block(2, 2, side, 2, rows, PAD),
+            block(ROWS, RANK),
             pltpu.SemaphoreType.DMA((6,)),
+            pltpu.SemaphoreType.DMA((4,)),
             pltpu.SemaphoreType.DMA((copies,)),
             pltpu.SemaphoreType.DMA((copies,)),
         ],
@@ -501,8 +540,16 @@
             jax.ShapeDtypeStruct((ROWS, RANK), BF16),
             jax.ShapeDtypeStruct((2, RANK, COLUMNS), F32),
         ),
-        in_specs=[vmem] * 3,
-        out_specs=(vmem,) * 5,
+        in_specs=[anywhere] * 3,
+        out_specs=(anywhere,) * 5,
+        scratch_shapes=[
+            block(3, 2, ROWS, PAIR),
+            block(2, 2, side, 2, rows, PAD),
+            block(3, ROWS, COLUMNS),
+            block(2, RANK, COLUMNS, dtype=F32),
+            pltpu.SemaphoreType.DMA((5,)),
+            pltpu.SemaphoreType.DMA((6,)),
+        ],
         compiler_params=pltpu.CompilerParams(vmem_limit_bytes=56 * 2**20),
     )(outs, grad_input, adapter)
 

time: 55.6 us -> 54 us (0.971)
  Pallas kernels: 54.7 us -> 53.2 us
    pallas_call x1, Pallas kernels: 52.1 us -> 50.7 us  [body(): pl.pallas_call(functools.partial(kernel, side, n_tp), out_shape=(jax.Shap...]
where the time goes in v3:
time: 54 us; the launch traced here: 53.8 us
  Pallas kernels  53.2 us (99%)
  between operations  0.64 us (1%)
    pallas_call x1, Pallas kernels, body(): pl.pallas_call(functools.partial(kernel, side, n_tp), out_shape=(jax.Shap...  50.7 us
    pallas_call x1, Pallas kernels, body(): pl.pallas_call(finish, out_shape=(jax.ShapeDtypeStruct((ROWS, COLUMNS), B...  2.45 us

profile of v3, /device:TPU:1, one launch (start us, length us, event | category | flops | bytes accessed | tf_op | source)
XLA Modules:
  0.0 53.8 jit_solution(3427943665971550447)
XLA Ops:
  0.6 50.7 %shard_map.119 = (bf16[3,2,128,512]{3,2,1,0:T(8,128)(2,1)}, bf16[128,128]{1,0:T(8,128)(2,1)}, bf16[2,2,8,2,16,256]{5,4,3,2,1,0:T(8,128)(2,1)}) custom-call(s32[256]{0:T(256)} %slot_ref.1, s32[256]{0:T(256)} %first_ref.1, bf16[128,896]{1,0:T(8,128)(2,1)} %q_hbm.1, bf16[128,896]{1,0:T(8,128)(2,1)} %k_hbm.1, bf16[128,896]{1,0:T(8,128)(2,1)} %v_hbm.1, ...), custom_call_target="tpu_custom_call" | custom-call | tf_op jit(solution)/shard_map/pallas_call | solution.py:484
  51.4 2.5 %shard_map.120 = (bf16[128,896]{1,0:T(8,128)(2,1)}, bf16[128,896]{1,0:T(8,128)(2,1)}, bf16[128,896]{1,0:T(8,128)(2,1)}, bf16[128,128]{1,0:T(8,128)(2,1)}, f32[2,128,896]{2,1,0:T(8,128)}) custom-call(bf16[3,2,128,512]{3,2,1,0:T(8,128)(2,1)} %get-tuple-element.8.out_hbm, bf16[128,128]{1,0:T(8,128)(2,1)} %get-tuple-element.9.gi_hbm, ...), custom_call_target="tpu_custom_call" | custom-call | tf_op jit(solution)/shard_map/pallas_call | solution.py:534

commit v4 on v3

--- a/solution.py
+++ b/solution.py
@@ -26,12 +26,12 @@
 S_KEY, S_VALUE, S_QUERY, S_GRAD, S_ACT = range(5)
 S_OUT = 5
 S_INPUT = 8
-S_ADAPTER = 9
-S_NEXT = 11
-S_BACK = 15
-S_PAST = 19
-S_FIRST = 21
-S_ALONG = 22
+S_NEXT = 9
+S_BACK = 13
+S_PAST = 17
+S_FIRST = 19
+S_ALONG = 20
+UNIT_AXIS = (0, 0, 1)
 MESH = pl.DeviceIdType.MESH
 F32 = jnp.float32
 BF16 = jnp.bfloat16
@@ -59,13 +59,18 @@
 def kernel(
     side, n_tp,
     slot_ref, first_ref, q_hbm, k_hbm, v_hbm, a_hbm, w_hbm, g_hbm,
-    out_hbm, gi_hbm, ga_hbm,
+    out_hbm, gi_hbm, ga0_hbm, ga1_hbm, ga2_hbm,
     raw, act, weight, weight_pad, packed, sibling, act_sib, act_past, act_window, key_past,
     window_kv, sorted_qg, probs, probs_low, back_send, back_recv, own_kv,
     grads, sib_send, outs, gi_send, gi_sib, gi_along,
-    part, scattered, crossed, gathered, gi_out,
-    load_sem, store_sem, send_sem, recv_sem,
+    part0, part1, part2, scattered0, scattered1, scattered2,
+    crossed0, crossed1, crossed2, gathered0, gathered1, gathered2, gi_out,
+    load_sem, store_sem, send_sem, recv_sem, entered_sem,
 ):
+    part = (part0, part1, part2)
+    scattered = (scattered0, scattered1, scattered2)
+    crossed = (crossed0, crossed1, crossed2)
+    gathered = (gathered0, gathered1, gathered2)
     me = lax.axis_index("ctx")
     tp = lax.axis_index("tp")
     core = lax.rem(me, 2)
@@ -103,7 +108,8 @@
         pl.semaphore_signal(barrier, inc=1, device_id=(ctx, x), device_id_type=MESH)
 
     steps = [side // 2 + (i // 2) * (1 - 2 * (i % 2)) for i in range(1, side)]
-    for step in steps:
+    near = [step for step in steps if min(step, side - step) <= 2]
+    for step in near:
         greet(along(0, step), tp)
         greet(along(1, step), tp)
     for step in range(1, n_tp):
@@ -151,7 +157,7 @@
     loads[0].wait()
     pack(KEY, padded(raw[KEY]))
     loads[1].wait()
-    pl.semaphore_wait(barrier, 5 + 2 * (side - 1) + n_tp - 1)
+    pl.semaphore_wait(barrier, 5 + 2 * len(near) + n_tp - 1)
     sib_key = to_sibling(KEY, S_KEY)
     sib_key.start()
     sib_act = remote(act, act_sib, S_ACT, other)
@@ -165,6 +171,9 @@
         copy.start()
     next_act = remote(act, act_past.at[core], S_PAST, after)
     next_act.start()
+    relays = [(axis, step) for axis in (0, 1) for step in (2, side - 2)] if len(near) < len(steps) else []
+    for axis, step in relays:
+        pl.semaphore_signal(entered_sem, inc=1, device_id=(along(axis, step), tp), device_id_type=MESH)
     loads[2].wait()
     for i in range(2):
         wide = padded(weight[i])
@@ -233,35 +242,46 @@
     visible = (key_place >= lowest) & (key_place <= query_place + GROUP_ROWS)
 
     def along_sem(unit, stage, step):
-        return S_ALONG + (unit * 3 + stage) * side + step
-
-    position = [(y, z), (z, y)]
+        return S_ALONG + (unit * 4 + stage) * side + step
+
+    def position(unit, crossing):
+        return (y, z)[UNIT_AXIS[unit] ^ crossing]
 
     def scatter(unit, step):
-        target = lax.rem(position[unit][0] + step, side)
+        target = lax.rem(position(unit, 0) + step, side)
         return remote(
-            part.at[unit, target], scattered.at[unit, step], along_sem(unit, 0, step), along(unit, step)
+            part[unit].at[target], scattered[unit].at[step], along_sem(unit, 0, step),
+            along(UNIT_AXIS[unit], step),
         )
 
     def cross(unit, step):
-        block = crossed.at[unit, position[unit][1]]
-        return remote(block, block, along_sem(unit, 1, step), along(1 - unit, step))
+        block = crossed[unit].at[position(unit, 1)]
+        return remote(block, block, along_sem(unit, 1, step), along(1 - UNIT_AXIS[unit], step))
 
     def gather(unit, step):
-        block = gathered.at[unit, core, position[unit][0]]
-        return remote(block, block, along_sem(unit, 2, step), along(unit, step))
-
-    def each(make, unit, method):
-        if method == "start":
-            for step in steps:
-                make(unit, step).start()
-            return
-
+        block = gathered[unit].at[core, position(unit, 0)]
+        return remote(block, block, along_sem(unit, 2, step), along(UNIT_AXIS[unit], step))
+
+    def gather_other(unit, step):
+        block = gathered[unit].at[core, position(unit, 0)]
+        target = along(UNIT_AXIS[unit], step) + 1 - 2 * core
+        return remote(block, block, along_sem(unit, 3, step), target)
+
+    def each(make, unit, method, first=1):
         def run(step, carry):
             getattr(make(unit, step), method)()
             return carry
 
-        lax.fori_loop(1, side, run, 0)
+        lax.fori_loop(first, side, run, 0)
+
+    def adapter_terms(block, activations, values):
+        terms = dot(activations, values, (0, 0)).astype(BF16)
+        for j in range(side):
+            block(j)[...] = terms[j * rows:(j + 1) * rows]
+
+    def send_unit(unit):
+        for step in steps:
+            scatter(unit, step).start()
 
     def back(kind, head):
         lanes = pl.ds(head * PAD, PAD)
@@ -301,9 +321,11 @@
             for i, values in enumerate(in_order(act_past[0], act_past[1], past_places)):
                 if i:
                     act_window[i * STRETCH:(i + 1) * STRETCH] = values
-        adapter = dot(act_window[...], terms, (0, 0)).astype(BF16)
-        for j in range(side):
-            part[head, j, 1] = adapter[j * rows:(j + 1) * rows]
+        if head:
+            adapter_terms(lambda j: part[1].at[j], act_window[...], terms)
+            send_unit(1)
+        else:
+            adapter_terms(lambda j: part[0].at[j, 1], act_window[...], terms)
 
         next_kv[VALUE, head].wait_recv()
         grad_probs = dot(window_kv[VALUE, :, lanes], sorted_qg[1, :, lanes], (1, 1))
@@ -311,10 +333,14 @@
         grad_scores = (probs[head] * (grad_probs - row_dot)).astype(BF16)
         summed = (dot(grad_scores, window_kv[KEY, :, lanes], (0, 0)) * SCALE).astype(BF16)
         grads[0, :, lanes] = summed
-        adapter = dot(act_window[GROUP_ROWS:], summed, (0, 0)).astype(BF16)
-        for j in range(side):
-            part[head, j, 0] = adapter[j * rows:(j + 1) * rows]
-        each(scatter, head, "start")
+        if head:
+            adapter_terms(lambda j: part[2].at[j], act_window[GROUP_ROWS:], summed)
+            send_unit(2)
+        else:
+            adapter_terms(lambda j: part[0].at[j, 0], act_window[GROUP_ROWS:], summed)
+            if relays:
+                pl.semaphore_wait(entered_sem, len(relays))
+            send_unit(0)
         terms = dot(grad_scores, sorted_qg[0, :, lanes], (1, 0)) * SCALE
         back_send[KEY, :, lanes] = terms[STRETCH:GROUP_ROWS].astype(BF16)
         own_kv[KEY, :, lanes] = terms[GROUP_ROWS:]
@@ -341,19 +367,23 @@
 
     def go_across(unit):
         each(scatter, unit, "wait_recv")
-        total = part[unit, position[unit][0]].astype(F32)
+        total = part[unit][position(unit, 0)].astype(F32)
         for step in range(1, side):
-            total = total + scattered[unit, step].astype(F32)
-        crossed[unit, position[unit][1]] = total.astype(BF16)
-        each(cross, unit, "start")
+            total = total + scattered[unit][step].astype(F32)
+        crossed[unit][position(unit, 1)] = total.astype(BF16)
+        for step in steps:
+            cross(unit, step).start()
 
     def go_around(unit):
         each(cross, unit, "wait_recv")
-        total = crossed[unit, 0].astype(F32)
+        total = crossed[unit][0].astype(F32)
         for step in range(1, side):
-            total = total + crossed[unit, step].astype(F32)
-        gathered[unit, core, position[unit][0]] = total.astype(BF16)
-        each(gather, unit, "start")
+            total = total + crossed[unit][step].astype(F32)
+        gathered[unit][core, position(unit, 0)] = total.astype(BF16)
+        for step in steps:
+            gather(unit, step).start()
+            gather_other(unit, step).start()
+        gather_other(unit, 0).start()
 
     input_part = input_terms(0, grads[0])
     out_query = hand_out(0, to_slots(grads[0]))
@@ -372,13 +402,14 @@
     out_value = hand_out(2, to_slots(grads[1]))
 
     go_across(1)
+    go_across(2)
 
     sib_input.wait_recv()
     gi_along[tp] = gi_along[tp] + gi_sib[...]
 
     def tp_copy(step):
         return remote(
-            gi_along.at[tp], gi_along.at[tp], S_ALONG + 6 * side + step, me, lax.rem(tp + step, n_tp)
+            gi_along.at[tp], gi_along.at[tp], S_ALONG + 12 * side + step, me, lax.rem(tp + step, n_tp)
         )
 
     def each_tp(method):
@@ -394,6 +425,7 @@
     out_key = hand_out(1, to_slots(add_back(KEY)))
 
     go_around(0)
+    go_around(1)
     each_tp("wait_recv")
     total = gi_along[0]
     for x in range(1, n_tp):
@@ -401,46 +433,43 @@
     gi_out[...] = total.astype(BF16)
     stores = [pltpu.make_async_copy(gi_out, gi_hbm, store_sem.at[0])]
     stores[0].start()
-    go_around(1)
+    go_around(2)
 
     for copy in (out_query, out_value, out_key):
         copy.wait_recv()
     stores.append(pltpu.make_async_copy(outs, out_hbm, store_sem.at[1]))
     stores[1].start()
 
-    sib_adapter = []
-    for unit in range(2):
-        each(gather, unit, "wait_recv")
-        block = gathered.at[unit, core]
-        copy = remote(block, block, S_ADAPTER + unit, other)
-        copy.start()
-        sib_adapter.append(copy)
-
     for copy in (
-        sib_key, sib_act, sib_value, sib_query, sib_grad, *next_first, next_act, pass_act, *next_kv.values(),
-        *backs.values(), out_query, out_value, out_key, sib_input,
+        sib_key, sib_act, sib_value, sib_query, sib_grad, *next_first, next_act, pass_act,
+        *next_kv.values(), *backs.values(), out_query, out_value, out_key, sib_input,
     ):
         copy.wait_send()
-    for unit in range(2):
+    each_tp("wait_send")
+    for unit in range(3):
         each(scatter, unit, "wait_send")
         each(cross, unit, "wait_send")
+    for unit, hbm in enumerate((ga0_hbm, ga1_hbm, ga2_hbm)):
+        each(gather, unit, "wait_recv")
+        each(gather_other, unit, "wait_recv", 0)
+        stores.append(pltpu.make_async_copy(gathered[unit], hbm, store_sem.at[2 + unit]))
+        stores[2 + unit].start()
+    for unit in range(3):
         each(gather, unit, "wait_send")
-    each_tp("wait_send")
-    for unit in range(2):
-        sib_adapter[unit].wait_recv()
-        stores.append(pltpu.make_async_copy(gathered.at[unit], ga_hbm.at[unit], store_sem.at[2 + unit]))
-        stores[2 + unit].start()
-        sib_adapter[unit].wait_send()
+        each(gather_other, unit, "wait_send", 0)
     for store in stores:
         store.wait()
 
 
 def finish(
-    out_hbm, gi_hbm, ga_hbm, q_hbm, k_hbm, v_hbm, input_hbm, adapter_hbm,
-    outs, gathered, wide, adapter, load_sem, store_sem,
+    out_hbm, gi_hbm, ga0_hbm, ga1_hbm, ga2_hbm, q_hbm, k_hbm, v_hbm, input_hbm, adapter_hbm,
+    outs, head0, value1, query1, wide, adapter, load_sem, store_sem,
 ):
     loads = [pltpu.make_async_copy(out_hbm.at[i], outs.at[i], load_sem.at[i]) for i in range(3)]
-    loads += [pltpu.make_async_copy(ga_hbm.at[i], gathered.at[i], load_sem.at[3 + i]) for i in range(2)]
+    loads += [
+        pltpu.make_async_copy(hbm, block, load_sem.at[3 + i])
+        for i, (hbm, block) in enumerate(((ga0_hbm, head0), (ga1_hbm, value1), (ga2_hbm, query1)))
+    ]
     for load in loads:
         load.start()
     stores = [
@@ -455,12 +484,12 @@
         wide[i] = unpadded([outs[i, 0], outs[i, 1]])
         stores[i].start()
     loads[3].wait()
-    loads[4].wait()
-    for i in range(2):
-        heads = [
-            gathered[unit, pair, :, i].reshape(RANK, PAD)[:, :HEAD].astype(F32)
-            for pair in range(2) for unit in range(2)
-        ]
+    for i, head1 in ((1, value1), (0, query1)):
+        loads[5 - i].wait()
+        heads = []
+        for pair in range(2):
+            heads += [head0[pair, :, i], head1[pair]]
+        heads = [head.reshape(RANK, PAD)[:, :HEAD].astype(F32) for head in heads]
         adapter[i] = jnp.concatenate(heads, axis=1)
         stores[3 + i].start()
     for store in stores:
@@ -474,22 +503,24 @@
     n_tp = lax.axis_size("tp")
     side = math.isqrt(lax.axis_size("ctx") // 2)
     rows = RANK // side
-    copies = S_ALONG + 6 * side + n_tp
+    copies = S_ALONG + 12 * side + n_tp
     anywhere = pl.BlockSpec(memory_space=pltpu.HBM)
     smem = pl.BlockSpec(memory_space=pltpu.SMEM)
 
     def block(*shape, dtype=BF16):
         return pltpu.VMEM(shape, dtype)
 
-    outs, grad_input, adapter = pl.pallas_call(
+    partial_results = pl.pallas_call(
         functools.partial(kernel, side, n_tp),
         out_shape=(
             jax.ShapeDtypeStruct((3, 2, ROWS, PAIR), BF16),
             jax.ShapeDtypeStruct((ROWS, RANK), BF16),
-            jax.ShapeDtypeStruct((2, 2, side, 2, rows, PAD), BF16),
+            jax.ShapeDtypeStruct((2, side, 2, rows, PAD), BF16),
+            jax.ShapeDtypeStruct((2, side, rows, PAD), BF16),
+            jax.ShapeDtypeStruct((2, side, rows, PAD), BF16),
         ),
         in_specs=[smem, smem] + [anywhere] * 6,
-        out_specs=(anywhere,) * 3,
+        out_specs=(anywhere,) * 5,
         scratch_shapes=[
             block(4, ROWS, COLUMNS),
             block(ROWS, RANK),
@@ -514,15 +545,16 @@
             block(ROWS, RANK, dtype=F32),
             block(ROWS, RANK, dtype=F32),
             block(n_tp, ROWS, RANK, dtype=F32),
+            *((block(side, 2, rows, PAD), block(side, rows, PAD), block(side, rows, PAD)) * 3),
             block(2, side, 2, rows, PAD),
-            block(2, side, 2, rows, PAD),
-            block(2, side, 2, rows, PAD),
-            block(2, 2, side, 2, rows, PAD),
+            block(2, side, rows, PAD),
+            block(2, side, rows, PAD),
             block(ROWS, RANK),
             pltpu.SemaphoreType.DMA((6,)),
-            pltpu.SemaphoreType.DMA((4,)),
+            pltpu.SemaphoreType.DMA((5,)),
             pltpu.SemaphoreType.DMA((copies,)),
             pltpu.SemaphoreType.DMA((copies,)),
+            pltpu.SemaphoreType.REGULAR,
         ],
         compiler_params=pltpu.CompilerParams(
             collective_id=0, has_side_effects=True, vmem_limit_bytes=56 * 2**20
@@ -540,18 +572,20 @@
             jax.ShapeDtypeStruct((ROWS, RANK), BF16),
             jax.ShapeDtypeStruct((2, RANK, COLUMNS), F32),
         ),
-        in_specs=[anywhere] * 3,
+        in_specs=[anywhere] * 5,
         out_specs=(anywhere,) * 5,
         scratch_shapes=[
             block(3, 2, ROWS, PAIR),
-            block(2, 2, side, 2, rows, PAD),
+            block(2, side, 2, rows, PAD),
+            block(2, side, rows, PAD),
+            block(2, side, rows, PAD),
             block(3, ROWS, COLUMNS),
             block(2, RANK, COLUMNS, dtype=F32),
-            pltpu.SemaphoreType.DMA((5,)),
+            pltpu.SemaphoreType.DMA((6,)),
             pltpu.SemaphoreType.DMA((6,)),
         ],
         compiler_params=pltpu.CompilerParams(vmem_limit_bytes=56 * 2**20),
-    )(outs, grad_input, adapter)
+    )(*partial_results)
 
 
 def solution(mesh):

time: 54 us -> 54.3 us (level)
  no operation moved by 1% of the time
where the time goes in v4:
time: 54.3 us; the launch traced here: 54.1 us
  Pallas kernels  53.5 us (99%)
  between operations  0.64 us (1%)
    pallas_call x1, Pallas kernels, body(): pl.pallas_call(functools.partial(kernel, side, n_tp), out_shape=(jax.Shap...  51 us
    pallas_call x1, Pallas kernels, body(): pl.pallas_call(finish, out_shape=(jax.ShapeDtypeStruct((ROWS, COLUMNS), B...  2.46 us

profile of v4, /device:TPU:1, one launch (start us, length us, event | category | flops | bytes accessed | tf_op | source)
XLA Modules:
  0.0 54.1 jit_solution(5541401693808726384)
XLA Ops:
  0.6 51.0 %shard_map.119 = (bf16[3,2,128,512]{3,2,1,0:T(8,128)(2,1)}, bf16[128,128]{1,0:T(8,128)(2,1)}, bf16[2,8,2,16,256]{4,3,2,1,0:T(8,128)(2,1)}, bf16[2,8,16,256]{3,2,1,0:T(8,128)(2,1)}, bf16[2,8,16,256]{3,2,1,0:T(8,128)(2,1)}) custom-call(s32[256]{0:T(256)} %slot_ref.1, s32[256]{0:T(256)} %first_ref.1, bf16[128,896]{1,0:T(8,128)(2,1)} %q_hbm.1, ...), custom_call_target="tpu_custom_call" | custom-call | tf_op jit(solution)/shard_map/pallas_call | solution.py:513
  51.7 2.5 %shard_map.120 = (bf16[128,896]{1,0:T(8,128)(2,1)}, bf16[128,896]{1,0:T(8,128)(2,1)}, bf16[128,896]{1,0:T(8,128)(2,1)}, bf16[128,128]{1,0:T(8,128)(2,1)}, f32[2,128,896]{2,1,0:T(8,128)}) custom-call(bf16[3,2,128,512]{3,2,1,0:T(8,128)(2,1)} %get-tuple-element.10.out_hbm, bf16[128,128]{1,0:T(8,128)(2,1)} %get-tuple-element.11.gi_hbm, ...), custom_call_target="tpu_custom_call" | custom-call | tf_op jit(solution)/shard_map/pallas_call | solution.py:566

commit v5 on v4

--- a/solution.py
+++ b/solution.py
@@ -30,7 +30,10 @@
 S_BACK = 13
 S_PAST = 17
 S_FIRST = 19
-S_ALONG = 20
+S_ADAPTER = 20
+S_ALONG = 23
+S_INPUTS = 32
+COPIES = 33
 UNIT_AXIS = (0, 0, 1)
 MESH = pl.DeviceIdType.MESH
 F32 = jnp.float32
@@ -241,38 +244,26 @@
         lowest = jnp.where(query_place >= i * STRETCH, start, lowest)
     visible = (key_place >= lowest) & (key_place <= query_place + GROUP_ROWS)
 
-    def along_sem(unit, stage, step):
-        return S_ALONG + (unit * 4 + stage) * side + step
-
     def position(unit, crossing):
         return (y, z)[UNIT_AXIS[unit] ^ crossing]
 
     def scatter(unit, step):
         target = lax.rem(position(unit, 0) + step, side)
         return remote(
-            part[unit].at[target], scattered[unit].at[step], along_sem(unit, 0, step),
-            along(UNIT_AXIS[unit], step),
+            part[unit].at[target], scattered[unit].at[step], S_ALONG + 3 * unit, along(UNIT_AXIS[unit], step)
         )
 
     def cross(unit, step):
         block = crossed[unit].at[position(unit, 1)]
-        return remote(block, block, along_sem(unit, 1, step), along(1 - UNIT_AXIS[unit], step))
+        return remote(block, block, S_ALONG + 3 * unit + 1, along(1 - UNIT_AXIS[unit], step))
 
     def gather(unit, step):
         block = gathered[unit].at[core, position(unit, 0)]
-        return remote(block, block, along_sem(unit, 2, step), along(UNIT_AXIS[unit], step))
-
-    def gather_other(unit, step):
-        block = gathered[unit].at[core, position(unit, 0)]
-        target = along(UNIT_AXIS[unit], step) + 1 - 2 * core
-        return remote(block, block, along_sem(unit, 3, step), target)
-
-    def each(make, unit, method, first=1):
-        def run(step, carry):
-            getattr(make(unit, step), method)()
-            return carry
-
-        lax.fori_loop(first, side, run, 0)
+        return remote(block, block, S_ALONG + 3 * unit + 2, along(UNIT_AXIS[unit], step))
+
+    def stage(unit, which):
+        block = scattered[unit].at[pl.ds(1, side - 1)]
+        return remote(block, block, S_ALONG + 3 * unit + which, other)
 
     def adapter_terms(block, activations, values):
         terms = dot(activations, values, (0, 0)).astype(BF16)
@@ -366,7 +357,7 @@
         ).astype(BF16)
 
     def go_across(unit):
-        each(scatter, unit, "wait_recv")
+        stage(unit, 0).wait_recv()
         total = part[unit][position(unit, 0)].astype(F32)
         for step in range(1, side):
             total = total + scattered[unit][step].astype(F32)
@@ -375,15 +366,13 @@
             cross(unit, step).start()
 
     def go_around(unit):
-        each(cross, unit, "wait_recv")
+        stage(unit, 1).wait_recv()
         total = crossed[unit][0].astype(F32)
         for step in range(1, side):
             total = total + crossed[unit][step].astype(F32)
         gathered[unit][core, position(unit, 0)] = total.astype(BF16)
         for step in steps:
             gather(unit, step).start()
-            gather_other(unit, step).start()
-        gather_other(unit, 0).start()
 
     input_part = input_terms(0, grads[0])
     out_query = hand_out(0, to_slots(grads[0]))
@@ -407,26 +396,18 @@
     sib_input.wait_recv()
     gi_along[tp] = gi_along[tp] + gi_sib[...]
 
-    def tp_copy(step):
-        return remote(
-            gi_along.at[tp], gi_along.at[tp], S_ALONG + 12 * side + step, me, lax.rem(tp + step, n_tp)
-        )
-
-    def each_tp(method):
-        def run(step, carry):
-            getattr(tp_copy(step), method)()
-            return carry
-
-        lax.fori_loop(1, n_tp, run, 0)
-
-    each_tp("start")
+    for step in range(1, n_tp):
+        block = gi_along.at[tp]
+        remote(block, block, S_INPUTS, me, lax.rem(tp + step, n_tp)).start()
+    block = gi_along.at[pl.ds(1, n_tp - 1)]
+    tp_inputs = remote(block, block, S_INPUTS, other)
     for head in range(2):
         backs[KEY, head].wait_recv()
     out_key = hand_out(1, to_slots(add_back(KEY)))
 
     go_around(0)
     go_around(1)
-    each_tp("wait_recv")
+    tp_inputs.wait_recv()
     total = gi_along[0]
     for x in range(1, n_tp):
         total = total + gi_along[x]
@@ -445,18 +426,23 @@
         *next_kv.values(), *backs.values(), out_query, out_value, out_key, sib_input,
     ):
         copy.wait_send()
-    each_tp("wait_send")
+    tp_inputs.wait_send()
+    sib_adapter = []
     for unit in range(3):
-        each(scatter, unit, "wait_send")
-        each(cross, unit, "wait_send")
+        stage(unit, 0).wait_send()
+        stage(unit, 1).wait_send()
+    for unit in range(3):
+        stage(unit, 2).wait_recv()
+        block = gathered[unit].at[core]
+        copy = remote(block, block, S_ADAPTER + unit, other)
+        copy.start()
+        sib_adapter.append(copy)
+        stage(unit, 2).wait_send()
     for unit, hbm in enumerate((ga0_hbm, ga1_hbm, ga2_hbm)):
-        each(gather, unit, "wait_recv")
-        each(gather_other, unit, "wait_recv", 0)
+        sib_adapter[unit].wait_recv()
         stores.append(pltpu.make_async_copy(gathered[unit], hbm, store_sem.at[2 + unit]))
         stores[2 + unit].start()
-    for unit in range(3):
-        each(gather, unit, "wait_send")
-        each(gather_other, unit, "wait_send", 0)
+        sib_adapter[unit].wait_send()
     for store in stores:
         store.wait()
 
@@ -503,7 +489,6 @@
     n_tp = lax.axis_size("tp")
     side = math.isqrt(lax.axis_size("ctx") // 2)
     rows = RANK // side
-    copies = S_ALONG + 12 * side + n_tp
     anywhere = pl.BlockSpec(memory_space=pltpu.HBM)
     smem = pl.BlockSpec(memory_space=pltpu.SMEM)
 
@@ -552,8 +537,8 @@
             block(ROWS, RANK),
             pltpu.SemaphoreType.DMA((6,)),
             pltpu.SemaphoreType.DMA((5,)),
-            pltpu.SemaphoreType.DMA((copies,)),
-            pltpu.SemaphoreType.DMA((copies,)),
+            pltpu.SemaphoreType.DMA((COPIES,)),
+            pltpu.SemaphoreType.DMA((COPIES,)),
             pltpu.SemaphoreType.REGULAR,
         ],
         compiler_params=pltpu.CompilerParams(

time: 54.3 us -> 51.9 us (0.956)
  Pallas kernels: 53.5 us -> 51.1 us
    pallas_call x1, Pallas kernels: 51 us -> 48.6 us  [body(): pl.pallas_call(functools.partial(kernel, side, n_tp), out_shape=(jax.Shap...]
where the time goes in v5:
time: 51.9 us; the launch traced here: 51.7 us
  Pallas kernels  51.1 us (98%)
  between operations  0.64 us (1%)
    pallas_call x1, Pallas kernels, body(): pl.pallas_call(functools.partial(kernel, side, n_tp), out_shape=(jax.Shap...  48.6 us
    pallas_call x1, Pallas kernels, body(): pl.pallas_call(finish, out_shape=(jax.ShapeDtypeStruct((ROWS, COLUMNS), B...  2.46 us

profile of v5, /device:TPU:1, one launch (start us, length us, event | category | flops | bytes accessed | tf_op | source)
XLA Modules:
  0.0 51.7 jit_solution(1923045487328531641)
XLA Ops:
  0.6 48.6 %shard_map.119 = (bf16[3,2,128,512]{3,2,1,0:T(8,128)(2,1)}, bf16[128,128]{1,0:T(8,128)(2,1)}, bf16[2,8,2,16,256]{4,3,2,1,0:T(8,128)(2,1)}, bf16[2,8,16,256]{3,2,1,0:T(8,128)(2,1)}, bf16[2,8,16,256]{3,2,1,0:T(8,128)(2,1)}) custom-call(s32[256]{0:T(256)} %slot_ref.1, s32[256]{0:T(256)} %first_ref.1, bf16[128,896]{1,0:T(8,128)(2,1)} %q_hbm.1, ...), custom_call_target="tpu_custom_call" | custom-call | tf_op jit(solution)/shard_map/pallas_call | solution.py:498
  49.3 2.5 %shard_map.120 = (bf16[128,896]{1,0:T(8,128)(2,1)}, bf16[128,896]{1,0:T(8,128)(2,1)}, bf16[128,896]{1,0:T(8,128)(2,1)}, bf16[128,128]{1,0:T(8,128)(2,1)}, f32[2,128,896]{2,1,0:T(8,128)}) custom-call(bf16[3,2,128,512]{3,2,1,0:T(8,128)(2,1)} %get-tuple-element.10.out_hbm, bf16[128,128]{1,0:T(8,128)(2,1)} %get-tuple-element.11.gi_hbm, ...), custom_call_target="tpu_custom_call" | custom-call | tf_op jit(solution)/shard_map/pallas_call | solution.py:551

commit v6 on v5

--- a/solution.py
+++ b/solution.py
@@ -34,7 +34,7 @@
 S_ALONG = 23
 S_INPUTS = 32
 COPIES = 33
-UNIT_AXIS = (0, 0, 1)
+UNIT_AXIS = (1, 1, 0)
 MESH = pl.DeviceIdType.MESH
 F32 = jnp.float32
 BF16 = jnp.bfloat16
@@ -62,13 +62,13 @@
 def kernel(
     side, n_tp,
     slot_ref, first_ref, q_hbm, k_hbm, v_hbm, a_hbm, w_hbm, g_hbm,
-    out_hbm, gi_hbm, ga0_hbm, ga1_hbm, ga2_hbm,
+    out_ref, gi_ref, ga0_ref, ga1_ref, ga2_ref,
     raw, act, weight, weight_pad, packed, sibling, act_sib, act_past, act_window, key_past,
     window_kv, sorted_qg, probs, probs_low, back_send, back_recv, own_kv,
     grads, sib_send, outs, gi_send, gi_sib, gi_along,
     part0, part1, part2, scattered0, scattered1, scattered2,
-    crossed0, crossed1, crossed2, gathered0, gathered1, gathered2, gi_out,
-    load_sem, store_sem, send_sem, recv_sem, entered_sem,
+    crossed0, crossed1, crossed2, gathered0, gathered1, gathered2,
+    load_sem, send_sem, recv_sem, entered_sem,
 ):
     part = (part0, part1, part2)
     scattered = (scattered0, scattered1, scattered2)
@@ -260,6 +260,11 @@
     def gather(unit, step):
         block = gathered[unit].at[core, position(unit, 0)]
         return remote(block, block, S_ALONG + 3 * unit + 2, along(UNIT_AXIS[unit], step))
+
+    def gather_other(unit, step):
+        block = gathered[unit].at[core, position(unit, 0)]
+        target = along(UNIT_AXIS[unit], step) + 1 - 2 * core
+        return remote(block, block, S_ADAPTER + unit, target)
 
     def stage(unit, which):
         block = scattered[unit].at[pl.ds(1, side - 1)]
@@ -373,6 +378,9 @@
         gathered[unit][core, position(unit, 0)] = total.astype(BF16)
         for step in steps:
             gather(unit, step).start()
+        if unit == 2:
+            for step in steps + [0]:
+                gather_other(unit, step).start()
 
     input_part = input_terms(0, grads[0])
     out_query = hand_out(0, to_slots(grads[0]))
@@ -411,15 +419,12 @@
     total = gi_along[0]
     for x in range(1, n_tp):
         total = total + gi_along[x]
-    gi_out[...] = total.astype(BF16)
-    stores = [pltpu.make_async_copy(gi_out, gi_hbm, store_sem.at[0])]
-    stores[0].start()
+    gi_ref[...] = total.astype(BF16)
     go_around(2)
 
     for copy in (out_query, out_value, out_key):
         copy.wait_recv()
-    stores.append(pltpu.make_async_copy(outs, out_hbm, store_sem.at[1]))
-    stores[1].start()
+    out_ref[...] = outs[...]
 
     for copy in (
         sib_key, sib_act, sib_value, sib_query, sib_grad, *next_first, next_act, pass_act,
@@ -435,49 +440,38 @@
         stage(unit, 2).wait_recv()
         block = gathered[unit].at[core]
         copy = remote(block, block, S_ADAPTER + unit, other)
-        copy.start()
+        if unit < 2:
+            copy.start()
         sib_adapter.append(copy)
         stage(unit, 2).wait_send()
-    for unit, hbm in enumerate((ga0_hbm, ga1_hbm, ga2_hbm)):
+    for unit, ref in enumerate((ga0_ref, ga1_ref, ga2_ref)):
         sib_adapter[unit].wait_recv()
-        stores.append(pltpu.make_async_copy(gathered[unit], hbm, store_sem.at[2 + unit]))
-        stores[2 + unit].start()
+        ref[...] = gathered[unit][...]
         sib_adapter[unit].wait_send()
-    for store in stores:
-        store.wait()
 
 
 def finish(
-    out_hbm, gi_hbm, ga0_hbm, ga1_hbm, ga2_hbm, q_hbm, k_hbm, v_hbm, input_hbm, adapter_hbm,
-    outs, head0, value1, query1, wide, adapter, load_sem, store_sem,
+    out_ref, gi_ref, head0, value1, query1, q_hbm, k_hbm, v_hbm, input_hbm, adapter_hbm,
+    wide, adapter, store_sem,
 ):
-    loads = [pltpu.make_async_copy(out_hbm.at[i], outs.at[i], load_sem.at[i]) for i in range(3)]
-    loads += [
-        pltpu.make_async_copy(hbm, block, load_sem.at[3 + i])
-        for i, (hbm, block) in enumerate(((ga0_hbm, head0), (ga1_hbm, value1), (ga2_hbm, query1)))
+    stores = [
+        pltpu.make_async_copy(source, hbm, store_sem.at[i])
+        for i, (source, hbm) in enumerate((
+            (wide.at[0], q_hbm), (wide.at[1], k_hbm), (wide.at[2], v_hbm),
+            (adapter.at[0], adapter_hbm.at[0]), (adapter.at[1], adapter_hbm.at[1]), (gi_ref, input_hbm),
+        ))
     ]
-    for load in loads:
-        load.start()
-    stores = [
-        pltpu.make_async_copy(wide.at[i], hbm, store_sem.at[i])
-        for i, hbm in enumerate((q_hbm, k_hbm, v_hbm))
-    ]
-    stores += [pltpu.make_async_copy(adapter.at[i], adapter_hbm.at[i], store_sem.at[3 + i]) for i in range(2)]
-    stores += [pltpu.make_async_copy(gi_hbm, input_hbm, store_sem.at[5])]
     stores[5].start()
-    for i in range(3):
-        loads[i].wait()
-        wide[i] = unpadded([outs[i, 0], outs[i, 1]])
-        stores[i].start()
-    loads[3].wait()
     for i, head1 in ((1, value1), (0, query1)):
-        loads[5 - i].wait()
         heads = []
         for pair in range(2):
             heads += [head0[pair, :, i], head1[pair]]
         heads = [head.reshape(RANK, PAD)[:, :HEAD].astype(F32) for head in heads]
         adapter[i] = jnp.concatenate(heads, axis=1)
         stores[3 + i].start()
+    for i in range(3):
+        wide[i] = unpadded([out_ref[i, 0], out_ref[i, 1]])
+        stores[i].start()
     for store in stores:
         store.wait()
 
@@ -490,6 +484,7 @@
     side = math.isqrt(lax.axis_size("ctx") // 2)
     rows = RANK // side
     anywhere = pl.BlockSpec(memory_space=pltpu.HBM)
+    vmem = pl.BlockSpec(memory_space=pltpu.VMEM)
     smem = pl.BlockSpec(memory_space=pltpu.SMEM)
 
     def block(*shape, dtype=BF16):
@@ -498,14 +493,14 @@
     partial_results = pl.pallas_call(
         functools.partial(kernel, side, n_tp),
         out_shape=(
-            jax.ShapeDtypeStruct((3, 2, ROWS, PAIR), BF16),
-            jax.ShapeDtypeStruct((ROWS, RANK), BF16),
-            jax.ShapeDtypeStruct((2, side, 2, rows, PAD), BF16),
-            jax.ShapeDtypeStruct((2, side, rows, PAD), BF16),
-            jax.ShapeDtypeStruct((2, side, rows, PAD), BF16),
+            pltpu.VMEM((3, 2, ROWS, PAIR), BF16),
+            pltpu.VMEM((ROWS, RANK), BF16),
+            pltpu.VMEM((2, side, 2, rows, PAD), BF16),
+            pltpu.VMEM((2, side, rows, PAD), BF16),
+            pltpu.VMEM((2, side, rows, PAD), BF16),
         ),
         in_specs=[smem, smem] + [anywhere] * 6,
-        out_specs=(anywhere,) * 5,
+        out_specs=(vmem,) * 5,
         scratch_shapes=[
             block(4, ROWS, COLUMNS),
             block(ROWS, RANK),
@@ -534,15 +529,13 @@
             block(2, side, 2, rows, PAD),
             block(2, side, rows, PAD),
             block(2, side, rows, PAD),
-            block(ROWS, RANK),
             pltpu.SemaphoreType.DMA((6,)),
-            pltpu.SemaphoreType.DMA((5,)),
             pltpu.SemaphoreType.DMA((COPIES,)),
             pltpu.SemaphoreType.DMA((COPIES,)),
             pltpu.SemaphoreType.REGULAR,
         ],
         compiler_params=pltpu.CompilerParams(
-            collective_id=0, has_side_effects=True, vmem_limit_bytes=56 * 2**20
+            collective_id=0, has_side_effects=True, vmem_limit_bytes=54 * 2**20
         ),
     )(
         slot_stretch, doc_first, query_base, key_base, value_base, adapter_activation,
@@ -557,19 +550,14 @@
             jax.ShapeDtypeStruct((ROWS, RANK), BF16),
             jax.ShapeDtypeStruct((2, RANK, COLUMNS), F32),
         ),
-        in_specs=[anywhere] * 5,
+        in_specs=[vmem] * 5,
         out_specs=(anywhere,) * 5,
         scratch_shapes=[
-            block(3, 2, ROWS, PAIR),
-            block(2, side, 2, rows, PAD),
-            block(2, side, rows, PAD),
-            block(2, side, rows, PAD),
             block(3, ROWS, COLUMNS),
             block(2, RANK, COLUMNS, dtype=F32),
             pltpu.SemaphoreType.DMA((6,)),
-            pltpu.SemaphoreType.DMA((6,)),
         ],
-        compiler_params=pltpu.CompilerParams(vmem_limit_bytes=56 * 2**20),
+        compiler_params=pltpu.CompilerParams(vmem_limit_bytes=32 * 2**20),
     )(*partial_results)
 
 

time: 51.9 us -> 48.9 us (0.942)
  Pallas kernels: 51.1 us -> 48.1 us
    pallas_call x1, Pallas kernels: 48.6 us -> 46.8 us  [body(): pl.pallas_call(functools.partial(kernel, side, n_tp), out_shape=(pltpu.VM...]
    pallas_call x1, Pallas kernels: 2.46 us -> 1.32 us  [body(): pl.pallas_call(finish, out_shape=(jax.ShapeDtypeStruct((ROWS, COLUMNS), B...]
where the time goes in v6:
time: 48.9 us; the launch traced here: 48.8 us
  Pallas kernels  48.1 us (98%)
  between operations  0.64 us (1%)
    pallas_call x1, Pallas kernels, body(): pl.pallas_call(functools.partial(kernel, side, n_tp), out_shape=(pltpu.VM...  46.8 us
    pallas_call x1, Pallas kernels, body(): pl.pallas_call(finish, out_shape=(jax.ShapeDtypeStruct((ROWS, COLUMNS), B...  1.32 us

profile of v6, /device:TPU:1, one launch (start us, length us, event | category | flops | bytes accessed | tf_op | source)
XLA Modules:
  0.0 48.8 jit_solution(9198743188978278101)
XLA Ops:
  0.6 46.8 %shard_map.119 = (bf16[3,2,128,512]{3,2,1,0:T(8,128)(2,1)S(1)}, bf16[128,128]{1,0:T(8,128)(2,1)S(1)}, bf16[2,8,2,16,256]{4,3,2,1,0:T(8,128)(2,1)S(1)}, bf16[2,8,...) custom-call(s32[256]{0:T(256)} %slot_ref.1, s32[256]{0:T(256)} %first_ref.1, bf16[128,896]{1,0:T(8,128)(2,1)} %q_hbm.1, ...), custom_call_target="tpu_custom_call" | custom-call | tf_op jit(solution)/shard_map/pallas_call | solution.py:493
  47.5 1.3 %shard_map.120 = (bf16[128,896]{1,0:T(8,128)(2,1)}, bf16[128,896]{1,0:T(8,128)(2,1)}, bf16[128,896]{1,0:T(8,128)(2,1)}, bf16[128,128]{1,0:T(8,128)(2,1)}, f32[2,128,896]{2,1,0:T(8,128)}) custom-call(bf16[3,2,128,512]{3,2,1,0:T(8,128)(2,1)S(1)} %get-tuple-element.10.out_ref, bf16[128,128]{1,0:T(8,128)(2,1)S(1)} %get-tuple-element.11.gi_ref, ...), custom_call_target="tpu_custom_call" | custom-call | tf_op jit(solution)/shard_map/pallas_call | solution.py:544

commit v7 on v6

--- a/solution.py
+++ b/solution.py
@@ -33,7 +33,8 @@
 S_ADAPTER = 20
 S_ALONG = 23
 S_INPUTS = 32
-COPIES = 33
+S_PARTS = 33
+COPIES = 34
 UNIT_AXIS = (1, 1, 0)
 MESH = pl.DeviceIdType.MESH
 F32 = jnp.float32
@@ -61,14 +62,14 @@
 
 def kernel(
     side, n_tp,
-    slot_ref, first_ref, q_hbm, k_hbm, v_hbm, a_hbm, w_hbm, g_hbm,
+    slot_hbm, first_hbm, q_hbm, k_hbm, v_hbm, a_hbm, w_hbm, g_hbm,
     out_ref, gi_ref, ga0_ref, ga1_ref, ga2_ref,
     raw, act, weight, weight_pad, packed, sibling, act_sib, act_past, act_window, key_past,
     window_kv, sorted_qg, probs, probs_low, back_send, back_recv, own_kv,
     grads, sib_send, outs, gi_send, gi_sib, gi_along,
     part0, part1, part2, scattered0, scattered1, scattered2,
     crossed0, crossed1, crossed2, gathered0, gathered1, gathered2,
-    load_sem, send_sem, recv_sem, entered_sem,
+    slot_ref, first_ref, load_sem, send_sem, recv_sem, entered_sem,
 ):
     part = (part0, part1, part2)
     scattered = (scattered0, scattered1, scattered2)
@@ -100,7 +101,7 @@
         pltpu.make_async_copy(src, dst, load_sem.at[i])
         for i, (src, dst) in enumerate([
             (k_hbm, raw.at[KEY]), (a_hbm, act), (w_hbm, weight), (v_hbm, raw.at[VALUE]),
-            (q_hbm, raw.at[QUERY]), (g_hbm, raw.at[GRAD]),
+            (q_hbm, raw.at[QUERY]), (g_hbm, raw.at[GRAD]), (slot_hbm, slot_ref), (first_hbm, first_ref),
         ])
     ]
     loads[0].start()
@@ -124,6 +125,53 @@
     for load in loads[1:]:
         load.start()
 
+    def pack(kind, values):
+        packed[kind, 0] = values[:, :PAIR]
+        packed[kind, 1] = values[:, PAIR:]
+
+    def to_sibling(kind, sem):
+        return remote(packed.at[kind, 1 - core], sibling.at[kind], sem, other)
+
+    loads[0].wait()
+    pack(KEY, padded(raw[KEY]))
+    loads[1].wait()
+    pl.semaphore_wait(barrier, 5 + 2 * len(near) + n_tp - 1)
+    sib_key = to_sibling(KEY, S_KEY)
+    sib_key.start()
+    sib_act = remote(act, act_sib, S_ACT, other)
+    sib_act.start()
+    share_rows = pl.ds(pl.multiple_of(tp * (ROWS // n_tp), ROWS // n_tp), ROWS // n_tp)
+    next_act = remote(act.at[share_rows], act_past.at[core, share_rows], S_PAST, after)
+    next_act.start()
+    first = pl.ds(0, PAD)
+    next_first = [
+        remote(packed.at[KEY, core, :, first], key_past.at[core], S_NEXT, after),
+        remote(packed.at[KEY, 1 - core, :, first], key_past.at[core], S_FIRST, after_other),
+    ]
+    for copy in next_first:
+        copy.start()
+    relays = [(axis, step) for axis in (0, 1) for step in (2, side - 2)] if len(near) < len(steps) else []
+    for axis, step in relays:
+        pl.semaphore_signal(entered_sem, inc=1, device_id=(along(axis, step), tp), device_id_type=MESH)
+    loads[2].wait()
+
+    def adapt(kind, i):
+        wide = padded(weight[i])
+        weight_pad[i, 0] = wide[:, :PAIR]
+        weight_pad[i, 1] = wide[:, PAIR:]
+        wide = padded(raw[kind])
+        for pair in range(2):
+            update = dot(act[...], weight_pad[i, pair], (1, 0))
+            base = wide[:, pair * PAIR:(pair + 1) * PAIR].astype(F32)
+            packed[kind, pair] = (base + update).astype(BF16)
+
+    loads[3].wait()
+    adapt(VALUE, 1)
+    sib_value = to_sibling(VALUE, S_VALUE)
+    sib_value.start()
+
+    loads[6].wait()
+    loads[7].wait()
     places = [
         slot_ref[2 * me] - 4 * chip, slot_ref[2 * me + 1] - 4 * chip,
         slot_ref[2 * other] - 4 * chip, slot_ref[2 * other + 1] - 4 * chip,
@@ -150,51 +198,6 @@
             result.append(picked)
         return result
 
-    def pack(kind, values):
-        packed[kind, 0] = values[:, :PAIR]
-        packed[kind, 1] = values[:, PAIR:]
-
-    def to_sibling(kind, sem):
-        return remote(packed.at[kind, 1 - core], sibling.at[kind], sem, other)
-
-    loads[0].wait()
-    pack(KEY, padded(raw[KEY]))
-    loads[1].wait()
-    pl.semaphore_wait(barrier, 5 + 2 * len(near) + n_tp - 1)
-    sib_key = to_sibling(KEY, S_KEY)
-    sib_key.start()
-    sib_act = remote(act, act_sib, S_ACT, other)
-    sib_act.start()
-    first = pl.ds(0, PAD)
-    next_first = [
-        remote(packed.at[KEY, core, :, first], key_past.at[core], S_NEXT, after),
-        remote(packed.at[KEY, 1 - core, :, first], key_past.at[core], S_FIRST, after_other),
-    ]
-    for copy in next_first:
-        copy.start()
-    next_act = remote(act, act_past.at[core], S_PAST, after)
-    next_act.start()
-    relays = [(axis, step) for axis in (0, 1) for step in (2, side - 2)] if len(near) < len(steps) else []
-    for axis, step in relays:
-        pl.semaphore_signal(entered_sem, inc=1, device_id=(along(axis, step), tp), device_id_type=MESH)
-    loads[2].wait()
-    for i in range(2):
-        wide = padded(weight[i])
-        weight_pad[i, 0] = wide[:, :PAIR]
-        weight_pad[i, 1] = wide[:, PAIR:]
-
-    def adapt(kind, i):
-        wide = padded(raw[kind])
-        for pair in range(2):
-            update = dot(act[...], weight_pad[i, pair], (1, 0))
-            base = wide[:, pair * PAIR:(pair + 1) * PAIR].astype(F32)
-            packed[kind, pair] = (base + update).astype(BF16)
-
-    loads[3].wait()
-    adapt(VALUE, 1)
-    sib_value = to_sibling(VALUE, S_VALUE)
-    sib_value.start()
-
     def spread(kind):
         window_kv[kind, :STRETCH] = jnp.zeros((STRETCH, PAIR), BF16)
         for i, values in enumerate(in_order(packed[kind, core], sibling[kind])):
@@ -225,6 +228,13 @@
     sib_grad = to_sibling(GRAD, S_GRAD)
     sib_grad.start()
 
+    next_act.wait_recv()
+    block = act_past.at[core, share_rows]
+    for step in range(1, n_tp):
+        remote(block, block, S_PARTS, me, lax.rem(tp + step, n_tp)).start()
+    block = act_past.at[core, pl.ds(0, ROWS - ROWS // n_tp)]
+    tp_acts = remote(block, block, S_PARTS, other)
+    pass_act = remote(act_past.at[core], act_past.at[core], S_PAST + 1, other)
     sib_act.wait_recv()
     for i, values in enumerate(in_order(act[...], act_sib[...])):
         act_window[GROUP_ROWS + i * STRETCH:GROUP_ROWS + (i + 1) * STRETCH] = values
@@ -232,9 +242,6 @@
         copy.wait_recv()
         for i, values in enumerate(in_order(packed[kind, core], sibling[kind])):
             sorted_qg[kind - QUERY, i * STRETCH:(i + 1) * STRETCH] = values
-    next_act.wait_recv()
-    pass_act = remote(act_past.at[core], act_past.at[core], S_PAST + 1, other)
-    pass_act.start()
 
     key_place = lax.broadcasted_iota(jnp.int32, (WINDOW, GROUP_ROWS), 0)
     query_place = lax.broadcasted_iota(jnp.int32, (1, GROUP_ROWS), 1)
@@ -311,17 +318,13 @@
         back_send[VALUE, :, lanes] = terms[STRETCH:GROUP_ROWS]
         backs[VALUE, head] = back(VALUE, head)
         backs[VALUE, head].start()
-        if not head:
-            pass_act.wait_recv()
-            act_window[:STRETCH] = jnp.zeros((STRETCH, RANK), BF16)
-            for i, values in enumerate(in_order(act_past[0], act_past[1], past_places)):
-                if i:
-                    act_window[i * STRETCH:(i + 1) * STRETCH] = values
         if head:
             adapter_terms(lambda j: part[1].at[j], act_window[...], terms)
             send_unit(1)
         else:
-            adapter_terms(lambda j: part[0].at[j, 1], act_window[...], terms)
+            first_terms = terms
+            tp_acts.wait_recv()
+            pass_act.start()
 
         next_kv[VALUE, head].wait_recv()
         grad_probs = dot(window_kv[VALUE, :, lanes], sorted_qg[1, :, lanes], (1, 1))
@@ -334,6 +337,12 @@
             send_unit(2)
         else:
             adapter_terms(lambda j: part[0].at[j, 0], act_window[GROUP_ROWS:], summed)
+            pass_act.wait_recv()
+            act_window[:STRETCH] = jnp.zeros((STRETCH, RANK), BF16)
+            for i, values in enumerate(in_order(act_past[0], act_past[1], past_places)):
+                if i:
+                    act_window[i * STRETCH:(i + 1) * STRETCH] = values
+            adapter_terms(lambda j: part[0].at[j, 1], act_window[...], first_terms)
             if relays:
                 pl.semaphore_wait(entered_sem, len(relays))
             send_unit(0)
@@ -427,7 +436,7 @@
     out_ref[...] = outs[...]
 
     for copy in (
-        sib_key, sib_act, sib_value, sib_query, sib_grad, *next_first, next_act, pass_act,
+        sib_key, sib_act, sib_value, sib_query, sib_grad, *next_first, next_act, tp_acts, pass_act,
         *next_kv.values(), *backs.values(), out_query, out_value, out_key, sib_input,
     ):
         copy.wait_send()
@@ -483,9 +492,9 @@
     n_tp = lax.axis_size("tp")
     side = math.isqrt(lax.axis_size("ctx") // 2)
     rows = RANK // side
+    stretches = slot_stretch.shape[0]
     anywhere = pl.BlockSpec(memory_space=pltpu.HBM)
     vmem = pl.BlockSpec(memory_space=pltpu.VMEM)
-    smem = pl.BlockSpec(memory_space=pltpu.SMEM)
 
     def block(*shape, dtype=BF16):
         return pltpu.VMEM(shape, dtype)
@@ -499,7 +508,7 @@
             pltpu.VMEM((2, side, rows, PAD), BF16),
             pltpu.VMEM((2, side, rows, PAD), BF16),
         ),
-        in_specs=[smem, smem] + [anywhere] * 6,
+        in_specs=[anywhere] * 8,
         out_specs=(vmem,) * 5,
         scratch_shapes=[
             block(4, ROWS, COLUMNS),
@@ -529,7 +538,9 @@
             block(2, side, 2, rows, PAD),
             block(2, side, rows, PAD),
             block(2, side, rows, PAD),
-            pltpu.SemaphoreType.DMA((6,)),
+            pltpu.SMEM((stretches,), jnp.int32),
+            pltpu.SMEM((stretches,), jnp.int32),
+            pltpu.SemaphoreType.DMA((8,)),
             pltpu.SemaphoreType.DMA((COPIES,)),
             pltpu.SemaphoreType.DMA((COPIES,)),
             pltpu.SemaphoreType.REGULAR,

time: 48.9 us -> 49.1 us (level)
  no operation moved by 1% of the time
where the time goes in v7:
time: 49.1 us; the launch traced here: 48.9 us
  Pallas kernels  48.3 us (98%)
  between operations  0.64 us (1%)
    pallas_call x1, Pallas kernels, body(): pl.pallas_call(functools.partial(kernel, side, n_tp), out_shape=(pltpu.VM...  47 us
    pallas_call x1, Pallas kernels, body(): pl.pallas_call(finish, out_shape=(jax.ShapeDtypeStruct((ROWS, COLUMNS), B...  1.32 us

profile of v7, /device:TPU:1, one launch (start us, length us, event | category | flops | bytes accessed | tf_op | source)
XLA Modules:
  0.0 48.9 jit_solution(10524419550754335482)
XLA Ops:
  0.6 47.0 %shard_map.119 = (bf16[3,2,128,512]{3,2,1,0:T(8,128)(2,1)S(1)}, bf16[128,128]{1,0:T(8,128)(2,1)S(1)}, bf16[2,8,2,16,256]{4,3,2,1,0:T(8,128)(2,1)S(1)}, bf16[2,8,...) custom-call(s32[256]{0:T(256)} %slot_hbm.1, s32[256]{0:T(256)} %first_hbm.1, bf16[128,896]{1,0:T(8,128)(2,1)} %q_hbm.1, ...), custom_call_target="tpu_custom_call" | custom-call | tf_op jit(solution)/shard_map/pallas_call | solution.py:502
  47.6 1.3 %shard_map.120 = (bf16[128,896]{1,0:T(8,128)(2,1)}, bf16[128,896]{1,0:T(8,128)(2,1)}, bf16[128,896]{1,0:T(8,128)(2,1)}, bf16[128,128]{1,0:T(8,128)(2,1)}, f32[2,128,896]{2,1,0:T(8,128)}) custom-call(bf16[3,2,128,512]{3,2,1,0:T(8,128)(2,1)S(1)} %get-tuple-element.10.out_ref, bf16[128,128]{1,0:T(8,128)(2,1)S(1)} %get-tuple-element.11.gi_ref, ...), custom_call_target="tpu_custom_call" | custom-call | tf_op jit(solution)/shard_map/pallas_call | solution.py:555

commit v8 on v7

--- a/solution.py
+++ b/solution.py
@@ -31,11 +31,11 @@
 S_PAST = 17
 S_FIRST = 19
 S_ADAPTER = 20
-S_ALONG = 23
-S_INPUTS = 32
-S_PARTS = 33
-COPIES = 34
-UNIT_AXIS = (1, 1, 0)
+S_ALONG = 24
+S_INPUTS = 36
+S_PARTS = 37
+COPIES = 38
+UNITS = 4
 MESH = pl.DeviceIdType.MESH
 F32 = jnp.float32
 BF16 = jnp.bfloat16
@@ -63,18 +63,13 @@
 def kernel(
     side, n_tp,
     slot_hbm, first_hbm, q_hbm, k_hbm, v_hbm, a_hbm, w_hbm, g_hbm,
-    out_ref, gi_ref, ga0_ref, ga1_ref, ga2_ref,
+    out_ref, gi_ref, ga_ref,
     raw, act, weight, weight_pad, packed, sibling, act_sib, act_past, act_window, key_past,
     window_kv, sorted_qg, probs, probs_low, back_send, back_recv, own_kv,
     grads, sib_send, outs, gi_send, gi_sib, gi_along,
-    part0, part1, part2, scattered0, scattered1, scattered2,
-    crossed0, crossed1, crossed2, gathered0, gathered1, gathered2,
+    part, scattered, crossed, gathered,
     slot_ref, first_ref, load_sem, send_sem, recv_sem, entered_sem,
 ):
-    part = (part0, part1, part2)
-    scattered = (scattered0, scattered1, scattered2)
-    crossed = (crossed0, crossed1, crossed2)
-    gathered = (gathered0, gathered1, gathered2)
     me = lax.axis_index("ctx")
     tp = lax.axis_index("tp")
     core = lax.rem(me, 2)
@@ -251,38 +246,32 @@
         lowest = jnp.where(query_place >= i * STRETCH, start, lowest)
     visible = (key_place >= lowest) & (key_place <= query_place + GROUP_ROWS)
 
-    def position(unit, crossing):
-        return (y, z)[UNIT_AXIS[unit] ^ crossing]
-
     def scatter(unit, step):
-        target = lax.rem(position(unit, 0) + step, side)
+        target = lax.rem(z + step, side)
         return remote(
-            part[unit].at[target], scattered[unit].at[step], S_ALONG + 3 * unit, along(UNIT_AXIS[unit], step)
+            part.at[unit, target], scattered.at[unit, step], S_ALONG + 3 * unit, along(1, step)
         )
 
     def cross(unit, step):
-        block = crossed[unit].at[position(unit, 1)]
-        return remote(block, block, S_ALONG + 3 * unit + 1, along(1 - UNIT_AXIS[unit], step))
+        block = crossed.at[unit, y]
+        return remote(block, block, S_ALONG + 3 * unit + 1, along(0, step))
 
     def gather(unit, step):
-        block = gathered[unit].at[core, position(unit, 0)]
-        return remote(block, block, S_ALONG + 3 * unit + 2, along(UNIT_AXIS[unit], step))
+        block = gathered.at[unit, core, z]
+        return remote(block, block, S_ALONG + 3 * unit + 2, along(1, step))
 
     def gather_other(unit, step):
-        block = gathered[unit].at[core, position(unit, 0)]
-        target = along(UNIT_AXIS[unit], step) + 1 - 2 * core
-        return remote(block, block, S_ADAPTER + unit, target)
+        block = gathered.at[unit, core, z]
+        return remote(block, block, S_ADAPTER + unit, along(1, step) + 1 - 2 * core)
 
     def stage(unit, which):
-        block = scattered[unit].at[pl.ds(1, side - 1)]
+        block = scattered.at[unit, pl.ds(1, side - 1)]
         return remote(block, block, S_ALONG + 3 * unit + which, other)
 
-    def adapter_terms(block, activations, values):
+    def send_unit(unit, activations, values):
         terms = dot(activations, values, (0, 0)).astype(BF16)
         for j in range(side):
-            block(j)[...] = terms[j * rows:(j + 1) * rows]
-
-    def send_unit(unit):
+            part[unit, j] = terms[j * rows:(j + 1) * rows]
         for step in steps:
             scatter(unit, step).start()
 
@@ -319,8 +308,7 @@
         backs[VALUE, head] = back(VALUE, head)
         backs[VALUE, head].start()
         if head:
-            adapter_terms(lambda j: part[1].at[j], act_window[...], terms)
-            send_unit(1)
+            send_unit(2, act_window[...], terms)
         else:
             first_terms = terms
             tp_acts.wait_recv()
@@ -333,19 +321,17 @@
         summed = (dot(grad_scores, window_kv[KEY, :, lanes], (0, 0)) * SCALE).astype(BF16)
         grads[0, :, lanes] = summed
         if head:
-            adapter_terms(lambda j: part[2].at[j], act_window[GROUP_ROWS:], summed)
-            send_unit(2)
+            send_unit(3, act_window[GROUP_ROWS:], summed)
         else:
-            adapter_terms(lambda j: part[0].at[j, 0], act_window[GROUP_ROWS:], summed)
+            if relays:
+                pl.semaphore_wait(entered_sem, len(relays))
+            send_unit(1, act_window[GROUP_ROWS:], summed)
             pass_act.wait_recv()
             act_window[:STRETCH] = jnp.zeros((STRETCH, RANK), BF16)
             for i, values in enumerate(in_order(act_past[0], act_past[1], past_places)):
                 if i:
                     act_window[i * STRETCH:(i + 1) * STRETCH] = values
-            adapter_terms(lambda j: part[0].at[j, 1], act_window[...], first_terms)
-            if relays:
-                pl.semaphore_wait(entered_sem, len(relays))
-            send_unit(0)
+            send_unit(0, act_window[...], first_terms)
         terms = dot(grad_scores, sorted_qg[0, :, lanes], (1, 0)) * SCALE
         back_send[KEY, :, lanes] = terms[STRETCH:GROUP_ROWS].astype(BF16)
         own_kv[KEY, :, lanes] = terms[GROUP_ROWS:]
@@ -372,27 +358,28 @@
 
     def go_across(unit):
         stage(unit, 0).wait_recv()
-        total = part[unit][position(unit, 0)].astype(F32)
+        total = part[unit, z].astype(F32)
         for step in range(1, side):
-            total = total + scattered[unit][step].astype(F32)
-        crossed[unit][position(unit, 1)] = total.astype(BF16)
+            total = total + scattered[unit, step].astype(F32)
+        crossed[unit, y] = total.astype(BF16)
         for step in steps:
             cross(unit, step).start()
 
     def go_around(unit):
         stage(unit, 1).wait_recv()
-        total = crossed[unit][0].astype(F32)
+        total = crossed[unit, 0].astype(F32)
         for step in range(1, side):
-            total = total + crossed[unit][step].astype(F32)
-        gathered[unit][core, position(unit, 0)] = total.astype(BF16)
+            total = total + crossed[unit, step].astype(F32)
+        gathered[unit, core, z] = total.astype(BF16)
         for step in steps:
             gather(unit, step).start()
-        if unit == 2:
+        if unit == UNITS - 1:
             for step in steps + [0]:
                 gather_other(unit, step).start()
 
     input_part = input_terms(0, grads[0])
     out_query = hand_out(0, to_slots(grads[0]))
+    go_across(1)
     go_across(0)
 
     for head in range(2):
@@ -407,8 +394,8 @@
     gi_along[tp, STRETCH:] = input_slots[1]
     out_value = hand_out(2, to_slots(grads[1]))
 
-    go_across(1)
     go_across(2)
+    go_across(3)
 
     sib_input.wait_recv()
     gi_along[tp] = gi_along[tp] + gi_sib[...]
@@ -418,18 +405,19 @@
         remote(block, block, S_INPUTS, me, lax.rem(tp + step, n_tp)).start()
     block = gi_along.at[pl.ds(1, n_tp - 1)]
     tp_inputs = remote(block, block, S_INPUTS, other)
+    go_around(1)
+    go_around(0)
     for head in range(2):
         backs[KEY, head].wait_recv()
     out_key = hand_out(1, to_slots(add_back(KEY)))
 
-    go_around(0)
-    go_around(1)
+    go_around(2)
     tp_inputs.wait_recv()
     total = gi_along[0]
     for x in range(1, n_tp):
         total = total + gi_along[x]
     gi_ref[...] = total.astype(BF16)
-    go_around(2)
+    go_around(3)
 
     for copy in (out_query, out_value, out_key):
         copy.wait_recv()
@@ -442,25 +430,25 @@
         copy.wait_send()
     tp_inputs.wait_send()
     sib_adapter = []
-    for unit in range(3):
+    for unit in range(UNITS):
         stage(unit, 0).wait_send()
         stage(unit, 1).wait_send()
-    for unit in range(3):
+    for unit in range(UNITS):
         stage(unit, 2).wait_recv()
-        block = gathered[unit].at[core]
+        block = gathered.at[unit, core]
         copy = remote(block, block, S_ADAPTER + unit, other)
-        if unit < 2:
+        if unit < UNITS - 1:
             copy.start()
         sib_adapter.append(copy)
         stage(unit, 2).wait_send()
-    for unit, ref in enumerate((ga0_ref, ga1_ref, ga2_ref)):
+    for unit in range(UNITS):
         sib_adapter[unit].wait_recv()
-        ref[...] = gathered[unit][...]
+        ga_ref[unit] = gathered[unit]
         sib_adapter[unit].wait_send()
 
 
 def finish(
-    out_ref, gi_ref, head0, value1, query1, q_hbm, k_hbm, v_hbm, input_hbm, adapter_hbm,
+    out_ref, gi_ref, ga_ref, q_hbm, k_hbm, v_hbm, input_hbm, adapter_hbm,
     wide, adapter, store_sem,
 ):
     stores = [
@@ -471,10 +459,8 @@
         ))
     ]
     stores[5].start()
-    for i, head1 in ((1, value1), (0, query1)):
-        heads = []
-        for pair in range(2):
-            heads += [head0[pair, :, i], head1[pair]]
+    for i in range(2):
+        heads = [ga_ref[2 * head + 1 - i, pair] for pair in range(2) for head in range(2)]
         heads = [head.reshape(RANK, PAD)[:, :HEAD].astype(F32) for head in heads]
         adapter[i] = jnp.concatenate(heads, axis=1)
         stores[3 + i].start()
@@ -504,12 +490,10 @@
         out_shape=(
             pltpu.VMEM((3, 2, ROWS, PAIR), BF16),
             pltpu.VMEM((ROWS, RANK), BF16),
-            pltpu.VMEM((2, side, 2, rows, PAD), BF16),
-            pltpu.VMEM((2, side, rows, PAD), BF16),
-            pltpu.VMEM((2, side, rows, PAD), BF16),
+            pltpu.VMEM((UNITS, 2, side, rows, PAD), BF16),
         ),
         in_specs=[anywhere] * 8,
-        out_specs=(vmem,) * 5,
+        out_specs=(vmem,) * 3,
         scratch_shapes=[
             block(4, ROWS, COLUMNS),
             block(ROWS, RANK),
@@ -534,10 +518,10 @@
             block(ROWS, RANK, dtype=F32),
             block(ROWS, RANK, dtype=F32),
             block(n_tp, ROWS, RANK, dtype=F32),
-            *((block(side, 2, rows, PAD), block(side, rows, PAD), block(side, rows, PAD)) * 3),
-            block(2, side, 2, rows, PAD),
-            block(2, side, rows, PAD),
-            block(2, side, rows, PAD),
+            block(UNITS, side, rows, PAD),
+            block(UNITS, side, rows, PAD),
+            block(UNITS, side, rows, PAD),
+            block(UNITS, 2, side, rows, PAD),
             pltpu.SMEM((stretches,), jnp.int32),
             pltpu.SMEM((stretches,), jnp.int32),
             pltpu.SemaphoreType.DMA((8,)),
@@ -561,7 +545,7 @@
             jax.ShapeDtypeStruct((ROWS, RANK), BF16),
             jax.ShapeDtypeStruct((2, RANK, COLUMNS), F32),
         ),
-        in_specs=[vmem] * 5,
+        in_specs=[vmem] * 3,
         out_specs=(anywhere,) * 5,
         scratch_shapes=[
             block(3, ROWS, COLUMNS),

time: 49.1 us -> 50.5 us (1.029)
  Pallas kernels: 48.3 us -> 49.7 us
    pallas_call x1, Pallas kernels: 47 us -> 48.4 us  [body(): pl.pallas_call(functools.partial(kernel, side, n_tp), out_shape=(pltpu.VM...]
where the time goes in v8:
time: 50.5 us; the launch traced here: 50.3 us
  Pallas kernels  49.7 us (98%)
  between operations  0.64 us (1%)
    pallas_call x1, Pallas kernels, body(): pl.pallas_call(functools.partial(kernel, side, n_tp), out_shape=(pltpu.VM...  48.4 us
    pallas_call x1, Pallas kernels, body(): pl.pallas_call(finish, out_shape=(jax.ShapeDtypeStruct((ROWS, COLUMNS), B...  1.32 us

profile of v8, /device:TPU:1, one launch (start us, length us, event | category | flops | bytes accessed | tf_op | source)
XLA Modules:
  0.0 50.3 jit_solution(1366568002374613989)
XLA Ops:
  0.6 48.4 %shard_map.119 = (bf16[3,2,128,512]{3,2,1,0:T(8,128)(2,1)S(1)}, bf16[128,128]{1,0:T(8,128)(2,1)S(1)}, bf16[4,2,8,16,256]{4,3,2,1,0:T(8,128)(2,1)S(1)}) custom-call(s32[256]{0:T(256)} %slot_hbm.1, s32[256]{0:T(256)} %first_hbm.1, bf16[128,896]{1,0:T(8,128)(2,1)} %q_hbm.1, bf16[128,896]{1,0:T(8,128)(2,1)} %k_hbm.1, bf16[128,896]{1,0:T(8,128)(2,1)} %v_hbm.1, ...), custom_call_target="tpu_custom_call" | custom-call | tf_op jit(solution)/shard_map/pallas_call | solution.py:488
  49.0 1.3 %shard_map.120 = (bf16[128,896]{1,0:T(8,128)(2,1)}, bf16[128,896]{1,0:T(8,128)(2,1)}, bf16[128,896]{1,0:T(8,128)(2,1)}, bf16[128,128]{1,0:T(8,128)(2,1)}, f32[2,128,896]{2,1,0:T(8,128)}) custom-call(bf16[3,2,128,512]{3,2,1,0:T(8,128)(2,1)S(1)} %get-tuple-element.8.out_ref, bf16[128,128]{1,0:T(8,128)(2,1)S(1)} %get-tuple-element.9.gi_ref, ...), custom_call_target="tpu_custom_call" | custom-call | tf_op jit(solution)/shard_map/pallas_call | solution.py:539

commit v9 on v7

--- a/solution.py
+++ b/solution.py
@@ -35,7 +35,7 @@
 S_INPUTS = 32
 S_PARTS = 33
 COPIES = 34
-UNIT_AXIS = (1, 1, 0)
+UNIT_AXIS = (1, 0, 0)
 MESH = pl.DeviceIdType.MESH
 F32 = jnp.float32
 BF16 = jnp.bfloat16

time: 49.1 us -> 47.8 us (0.974)
  Pallas kernels: 48.3 us -> 47 us
    pallas_call x1, Pallas kernels: 47 us -> 45.7 us  [body(): pl.pallas_call(functools.partial(kernel, side, n_tp), out_shape=(pltpu.VM...]
where the time goes in v9:
time: 47.8 us; the launch traced here: 47.7 us
  Pallas kernels  47 us (98%)
  between operations  0.64 us (1%)
    pallas_call x1, Pallas kernels, body(): pl.pallas_call(functools.partial(kernel, side, n_tp), out_shape=(pltpu.VM...  45.7 us
    pallas_call x1, Pallas kernels, body(): pl.pallas_call(finish, out_shape=(jax.ShapeDtypeStruct((ROWS, COLUMNS), B...  1.32 us

profile of v9, /device:TPU:1, one launch (start us, length us, event | category | flops | bytes accessed | tf_op | source)
XLA Modules:
  0.0 47.7 jit_solution(10911949202114390443)
XLA Ops:
  0.6 45.7 %shard_map.119 = (bf16[3,2,128,512]{3,2,1,0:T(8,128)(2,1)S(1)}, bf16[128,128]{1,0:T(8,128)(2,1)S(1)}, bf16[2,8,2,16,256]{4,3,2,1,0:T(8,128)(2,1)S(1)}, bf16[2,8,...) custom-call(s32[256]{0:T(256)} %slot_hbm.1, s32[256]{0:T(256)} %first_hbm.1, bf16[128,896]{1,0:T(8,128)(2,1)} %q_hbm.1, ...), custom_call_target="tpu_custom_call" | custom-call | tf_op jit(solution)/shard_map/pallas_call | solution.py:502
  46.4 1.3 %shard_map.120 = (bf16[128,896]{1,0:T(8,128)(2,1)}, bf16[128,896]{1,0:T(8,128)(2,1)}, bf16[128,896]{1,0:T(8,128)(2,1)}, bf16[128,128]{1,0:T(8,128)(2,1)}, f32[2,128,896]{2,1,0:T(8,128)}) custom-call(bf16[3,2,128,512]{3,2,1,0:T(8,128)(2,1)S(1)} %get-tuple-element.10.out_ref, bf16[128,128]{1,0:T(8,128)(2,1)S(1)} %get-tuple-element.11.gi_ref, ...), custom_call_target="tpu_custom_call" | custom-call | tf_op jit(solution)/shard_map/pallas_call | solution.py:555

commit v10 on v9

--- a/solution.py
+++ b/solution.py
@@ -320,13 +320,14 @@
         backs[VALUE, head].start()
         if head:
             adapter_terms(lambda j: part[1].at[j], act_window[...], terms)
-            send_unit(1)
         else:
             first_terms = terms
             tp_acts.wait_recv()
             pass_act.start()
 
         next_kv[VALUE, head].wait_recv()
+        if head:
+            send_unit(1)
         grad_probs = dot(window_kv[VALUE, :, lanes], sorted_qg[1, :, lanes], (1, 1))
         row_dot = jnp.sum(probs_low[head].astype(F32) * grad_probs, axis=0, keepdims=True)
         grad_scores = (probs[head] * (grad_probs - row_dot)).astype(BF16)

time: 47.8 us -> 47.8 us (level)
  no operation moved by 1% of the time
where the time goes in v10:
time: 47.8 us; the launch traced here: 47.7 us
  Pallas kernels  47 us (98%)
  between operations  0.64 us (1%)
    pallas_call x1, Pallas kernels, body(): pl.pallas_call(functools.partial(kernel, side, n_tp), out_shape=(pltpu.VM...  45.7 us
    pallas_call x1, Pallas kernels, body(): pl.pallas_call(finish, out_shape=(jax.ShapeDtypeStruct((ROWS, COLUMNS), B...  1.32 us

profile of v10, /device:TPU:1, one launch (start us, length us, event | category | flops | bytes accessed | tf_op | source)
XLA Modules:
  0.0 47.7 jit_solution(1614366368316685739)
XLA Ops:
  0.6 45.7 %shard_map.119 = (bf16[3,2,128,512]{3,2,1,0:T(8,128)(2,1)S(1)}, bf16[128,128]{1,0:T(8,128)(2,1)S(1)}, bf16[2,8,2,16,256]{4,3,2,1,0:T(8,128)(2,1)S(1)}, bf16[2,8,...) custom-call(s32[256]{0:T(256)} %slot_hbm.1, s32[256]{0:T(256)} %first_hbm.1, bf16[128,896]{1,0:T(8,128)(2,1)} %q_hbm.1, ...), custom_call_target="tpu_custom_call" | custom-call | tf_op jit(solution)/shard_map/pallas_call | solution.py:503
  46.4 1.3 %shard_map.120 = (bf16[128,896]{1,0:T(8,128)(2,1)}, bf16[128,896]{1,0:T(8,128)(2,1)}, bf16[128,896]{1,0:T(8,128)(2,1)}, bf16[128,128]{1,0:T(8,128)(2,1)}, f32[2,128,896]{2,1,0:T(8,128)}) custom-call(bf16[3,2,128,512]{3,2,1,0:T(8,128)(2,1)S(1)} %get-tuple-element.10.out_ref, bf16[128,128]{1,0:T(8,128)(2,1)S(1)} %get-tuple-element.11.gi_ref, ...), custom_call_target="tpu_custom_call" | custom-call | tf_op jit(solution)/shard_map/pallas_call | solution.py:556
